TPU v7x, 32 devices: a whole 2x2x4 slice. The times are simulated.
32 devices in a mesh: gx: 2 (over core), gy: 4 (over y, x), gz: 4 (over z).
Axes of the slice: x: 2, y: 2, z: 4, core: 2. Of those that a mesh axis runs over, the one named last changes fastest.
Arguments:
- latent: bfloat16 [16, 64, 64, 256], P('gx', 'gy', 'gz'), may hold values from -700 to 700
- norm_gain: float32 [256], replicated, may hold values from 0.5 to 1.5
- norm_shift: float32 [256], replicated, may hold values from -3 to 3
- w_qkv: bfloat16 [256, 768], replicated, may hold values from -40 to 40
- w_out: bfloat16 [256, 256], replicated, may hold values from -0.375 to 0.375
- b_out: float32 [256], replicated, may hold values from -3 to 3
- depth_limit: int32 [4, 16, 16], P('gx', 'gy', 'gz'), may hold values from 0 to 1
Outputs:
- attended_out: bfloat16 [16, 64, 64, 256], P('gx', 'gy', 'gz')
All inputs are finite; a program needn't handle non-finite values.
Results may differ from a plain program's by a relative error of at most 0.038.
Values may be sent and summed in bfloat16 or wider, within the bound.
A program may use at most 128 MiB of HBM per device.

v0:
```python
import jax
import jax.numpy as jnp
import numpy as np
from jax import lax
from jax.sharding import PartitionSpec as P

HEADS = 8
GROUPS = 32


neighbour_offsets = [
    (first, second, third) for first in range(3) for second in range(3) for third in range(3)
]


def padded_2(cells, sides, width):
    for axis, dim in sides:
        count = lax.axis_size(axis)
        ends = count - 1
        head = lax.slice_in_dim(cells, 0, width, axis=dim)
        tail = lax.slice_in_dim(cells, cells.shape[dim] - width, cells.shape[dim], axis=dim)
        cells = jnp.concatenate(
            [
                lax.ppermute(tail, axis, [(i, (i + 1) % count) for i in range(ends)]),
                cells,
                lax.ppermute(head, axis, [((i + 1) % count, i) for i in range(ends)]),
            ],
            axis=dim,
        )
    return cells


def to_blocks(field):
    size_x, size_y, size_z, chans = field.shape
    shaped = field.reshape(size_x // 4, 4, size_y // 4, 4, size_z // 4, 4, chans)
    return shaped.transpose(0, 2, 4, 1, 3, 5, 6).reshape(
        size_x // 4, size_y // 4, size_z // 4, 64, chans
    )


def from_blocks(blocks):
    count_x, count_y, count_z, cells, chans = blocks.shape
    shaped = blocks.reshape(count_x, count_y, count_z, 4, 4, 4, chans)
    return shaped.transpose(0, 3, 1, 4, 2, 5, 6).reshape(
        count_x * 4, count_y * 4, count_z * 4, chans
    )


def valid_table(limit, start_x, start_y, start_z, total_x, total_y, total_z):
    table = jnp.asarray(np.array(neighbour_offsets, dtype=np.int32) - 1)
    index_x = start_x + jnp.arange(limit.shape[0], dtype=jnp.int32)
    index_y = start_y + jnp.arange(limit.shape[1], dtype=jnp.int32)
    index_z = start_z + jnp.arange(limit.shape[2], dtype=jnp.int32)
    key_x = index_x[:, None] + table[None, :, 0]
    key_y = index_y[:, None] + table[None, :, 1]
    key_z = index_z[:, None] + table[None, :, 2]
    inside_x = (key_x >= 0) & (key_x < total_x)
    inside_y = (key_y >= 0) & (key_y < total_y)
    inside_z = (key_z >= 0) & (key_z < total_z)
    depth_ok = jnp.abs(table[:, 2])[None, None, None, :] <= limit[..., None]
    return (
        inside_x[:, None, None, :]
        & inside_y[None, :, None, :]
        & inside_z[None, None, :, :]
        & depth_ok
    )


def attend_span(query_blocks, region, valid, heads):
    depth = query_blocks.shape[1]
    width = query_blocks.shape[-1]
    head_dim = width // heads
    pieces = [
        region[first, second : second + 2, third : third + depth]
        for first, second, third in neighbour_offsets
    ]
    keyvals = jnp.stack(pieces, axis=2).reshape(2, depth, 27 * 64, 2 * width)
    keys = keyvals[..., :width].reshape(2, depth, 27 * 64, heads, head_dim)
    values = keyvals[..., width:].reshape(2, depth, 27 * 64, heads, head_dim)
    queries = query_blocks.reshape(2, depth, 64, heads, head_dim)
    scores = jnp.einsum(
        "abqhd,abkhd->abhqk", queries, keys, preferred_element_type=jnp.float32
    ) * head_dim ** (-0.5)
    allowed = jnp.repeat(valid, 64, axis=-1)
    scores = jnp.where(allowed[:, :, None, None, :], scores, jnp.float32(-1e30))
    top = jnp.max(scores, axis=-1, keepdims=True)
    expd = jnp.exp(scores - top)
    weights = (expd / jnp.sum(expd, axis=-1, keepdims=True)).astype(jnp.bfloat16)
    mixed = jnp.einsum("abhqk,abkhd->abqhd", weights, values, preferred_element_type=jnp.float32)
    return mixed.astype(jnp.bfloat16).reshape(2, depth, 64, width)


def attend_all(query_blocks, kv_blocks, valid, heads):
    count_x, count_y, count_z = query_blocks.shape[:3]
    width = query_blocks.shape[-1]
    pairs = count_y // 2
    zero = jnp.zeros((), jnp.int32)

    def one_span(index):
        block_x = index // pairs
        block_y = index % pairs * 2
        query_part = lax.dynamic_slice(
            query_blocks, (block_x, block_y, zero, zero, zero), (1, 2, count_z, 64, width)
        )[0]
        region = lax.dynamic_slice(
            kv_blocks, (block_x, block_y, zero, zero, zero), (3, 4, count_z + 2, 64, 2 * width)
        )
        valid_part = lax.dynamic_slice(valid, (block_x, block_y, zero, zero), (1, 2, count_z, 27))[
            0
        ]
        return attend_span(query_part, region, valid_part, heads)

    result = lax.map(one_span, jnp.arange(count_x * pairs, dtype=jnp.int32))
    return result.reshape(count_x, count_y, count_z, 64, width)


def on_device(latent, norm_gain, norm_shift, w_qkv, w_out, b_out, depth_limit):
    size_x, size_y, size_z, width = latent.shape
    grouped = latent.astype(jnp.float32).reshape(-1, GROUPS, width // GROUPS)
    count = (
        grouped.shape[0]
        * grouped.shape[2]
        * lax.axis_size("gx")
        * lax.axis_size("gy")
        * lax.axis_size("gz")
    )
    mean = lax.psum(jnp.sum(grouped, axis=(0, 2)), ("gx", "gy", "gz")) / count
    centred = grouped - mean[None, :, None]
    var = lax.psum(jnp.sum(centred * centred, axis=(0, 2)), ("gx", "gy", "gz")) / count
    normed = (centred * lax.rsqrt(var + 1e-06)[None, :, None]).reshape(
        size_x, size_y, size_z, width
    )
    normed = (normed * norm_gain + norm_shift).astype(jnp.bfloat16)
    qkv = jnp.dot(normed.reshape(-1, width), w_qkv, preferred_element_type=jnp.float32).astype(
        jnp.bfloat16
    )
    queries = qkv[:, :width].reshape(size_x, size_y, size_z, width)
    keyvals = qkv[:, width:].reshape(size_x, size_y, size_z, 2 * width)
    padded = padded_2(keyvals, (("gx", 0), ("gy", 1), ("gz", 2)), 4)
    count_x, count_y, count_z = depth_limit.shape
    valid = valid_table(
        depth_limit,
        lax.axis_index("gx") * count_x,
        lax.axis_index("gy") * count_y,
        lax.axis_index("gz") * count_z,
        count_x * lax.axis_size("gx"),
        count_y * lax.axis_size("gy"),
        count_z * lax.axis_size("gz"),
    )
    mixed = from_blocks(attend_all(to_blocks(queries), to_blocks(padded), valid, HEADS))
    output = jnp.dot(mixed.reshape(-1, width), w_out, preferred_element_type=jnp.float32) + b_out
    return output.astype(jnp.bfloat16).reshape(size_x, size_y, size_z, width)


def solution(mesh):
    placed = (P("gx", "gy", "gz", None), P(), P(), P(), P(), P(), P("gx", "gy", "gz"))
    return jax.shard_map(
        on_device, mesh=mesh, in_specs=placed, out_specs=P("gx", "gy", "gz", None), check_vma=False
    )
```

profile of v0, /device:TPU:0, one launch (start us, length us, event | category | flops | bytes accessed | tf_op | source)
XLA Modules:
  0.0 714.9 jit_solution(7028842310895392550)
XLA Ops:
  1.8 42.0 %psum.14 = f32[32]{0:T(128)S(1)} all-reduce(f32[32]{0:T(128)S(1)} %reduce_sum.46), channel_id=1, replica_groups=mesh['gx'=2,'gy'=4,'gz'=4] {'gx','gy','gz'}, use_global_device_ids=true, to_apply=%region_2.0 | all-reduce | flops 32 | bytes 256 | tf_op jit(solution)/shard_map/psum | solution.py:127
  45.7 40.2 %psum.15 = f32[32]{0:T(128)S(1)} all-reduce(f32[32]{0:T(128)S(1)} %reduce_sum.49), channel_id=1, replica_groups=mesh['gx'=2,'gy'=4,'gz'=4] {'gx','gy','gz'}, use_global_device_ids=true, to_apply=%region_5.6 | all-reduce | flops 32 | bytes 256 | tf_op jit(solution)/shard_map/psum | solution.py:129
  100.8 21.3 %collective-permute-done.2 = bf16[16,4,16,512]{3,2,1,0:T(8,128)(2,1)S(1)} collective-permute-done((bf16[16,4,16,512]{3,2,1,0:T(8,128)(2,1)S(1)}, bf16[16,4,16,512]{3,2,1,0:T(8,128)(2,1)S(1)}, u32[]{:S(2)}, u32[]{:S(2)}) %collective-permute-start.2) | collective-permute-done | bytes 1048608 | tf_op jit(solution)/shard_map/ppermute | solution.py:24
  122.1 24.4 %collective-permute-done.3 = bf16[16,4,16,512]{3,2,1,0:T(8,128)(2,1)S(1)} collective-permute-done((bf16[16,4,16,512]{3,2,1,0:T(8,128)(2,1)S(1)}, bf16[16,4,16,512]{3,2,1,0:T(8,128)(2,1)S(1)}, u32[]{:S(2)}, u32[]{:S(2)}) %collective-permute-start.3) | collective-permute-done | bytes 1048608 | tf_op jit(solution)/shard_map/ppermute | solution.py:26
  161.1 24.4 %collective-permute-done.4 = bf16[16,24,4,512]{3,2,1,0:T(4,128)(2,1)} collective-permute-done((bf16[16,24,4,512]{3,2,1,0:T(4,128)(2,1)}, bf16[16,24,4,512]{3,2,1,0:T(4,128)(2,1)}, u32[]{:S(2)}, u32[]{:S(2)}) %collective-permute-start.4) | collective-permute-done | bytes 1572896 | tf_op jit(solution)/shard_map/ppermute | solution.py:24
  190.8 10.5 %pad_maximum_fusion = bf16[16,24,24,512]{3,2,1,0:T(8,128)(2,1)} fusion(bf16[16,24,4,512]{3,2,1,0:T(4,128)(2,1)} %collective-permute-done.5, bf16[16,4,16,512]{3,2,1,0:T(8,128)(2,1)} %copy-done.4, bf16[4,16,16,512]{3,2,1,0:T(8,128)(2,1)} %copy-done.2, bf16[8,16,16,512]{3,2,1,0:T(8,128)(2,1)S(1)} %bitcast.275, ...), kind=kLoop, calls=%fused_computation.71 | loop fusion | flops 66060288 | bytes 18874368 | tf_op jit(solution)/shard_map/concatenate | solution.py:22
  201.3 14.0 %reshape.177 = bf16[4,4,6,4,6,4,512]{6,5,4,3,2,1,0:T(4,128)(2,1)} reshape(bf16[16,24,24,512]{3,2,1,0:T(8,128)(2,1)} %pad_maximum_fusion) | data formatting | bytes 18874368 | tf_op jit(solution)/shard_map/reshape | solution.py:35
  215.3 21.7 %copy.72 = bf16[4,6,6,4,4,4,512]{6,0,5,4,3,2,1:T(4,128)(2,1)} copy(bf16[4,6,6,4,4,4,512]{6,5,2,4,1,3,0:T(4,128)(2,1)} %bitcast.271) | data formatting | bytes 18874368 | tf_op jit(solution)/shard_map/transpose | solution.py:36
  246.8 465.8 %while.12 = (s32[]{:T(128)}, bf16[4,2,4,64,256]{4,2,3,1,0:T(4,128)(2,1)S(1)}, s32[4]{0:T(128)S(1)}, bf16[4,6,6,64,512]{4,3,2,1,0:T(8,128)(2,1)}, pred[2,4,4,27]{...) while((s32[]{:T(128)}, ...), condition=%wide.region_9.10_spmd, body=%wide.region_6.9_spmd.sunk | while | flops 948569856 | bytes 158424544 | solution.py:113
  301.1 10.1 %fusion.124 = (bf16[2,4,1728,256]{3,2,1,0:T(8,128)(2,1)}, bf16[2,4,1728,256]{3,2,1,0:T(8,128)(2,1)}) fusion(bf16[2,4,1728,512]{3,2,1,0:T(8,128)(2,1)} %bitcast.268), kind=kLoop, calls=%fused_computation.105.clone.1 | loop fusion | bytes 28311552 | tf_op jit(solution)/shard_map/while/body/eval_jaxpr/slice | solution.py:78
  311.1 10.0 %copy.87 = bf16[2,4,1728,256]{2,3,1,0:T(8,128)(2,1)} copy(bf16[2,4,1728,256]{3,2,1,0:T(8,128)(2,1)} %get-tuple-element.162) | data formatting | bytes 14155776 | tf_op jit(solution)/shard_map/while/body/eval_jaxpr/slice | solution.py:78
  322.7 16.7 %fusion.126 = (f32[2,4,8,64]{3,2,1,0:T(8,128)S(1)}, f32[2,4,8,64,1728]{4,3,2,1,0:T(8,128)}) fusion(pred[2,4,1728]{2,1,0:T(4,128)(4,1)S(1)} %broadcast_in_dim.76, bf16[2,4,64,8,32]{2,4,3,1,0:T(8,128)(2,1)S(1)} %bitcast.276, bf16[2,4,1728,8,32]{2,4,3,1,0:T(8,128)(2,1)} %bitcast.269), kind=kOutput, calls=%fused_computation.106.clone.1 | convolution fusion | flops 481298112 | bytes 35681792 | tf_op jit(solution)/shard_map/while/body/eval_jaxpr/sub | solution.py:87
  339.4 10.0 %copy.85 = bf16[2,4,1728,256]{2,3,1,0:T(8,128)(2,1)} copy(bf16[2,4,1728,256]{3,2,1,0:T(8,128)(2,1)} %get-tuple-element.161) | data formatting | bytes 14155776 | tf_op jit(solution)/shard_map/while/body/eval_jaxpr/slice | solution.py:79
  349.4 13.6 %fusion.127 = bf16[2,4,8,32,64]{4,3,2,1,0:T(8,128)(2,1)S(1)} fusion(bf16[2,4,1728,8,32]{2,4,3,1,0:T(8,128)(2,1)} %bitcast.270, f32[2,4,8,64,1728]{4,3,2,1,0:T(8,128)} %get-tuple-element.163, f32[2,4,8,64]{3,2,1,0:T(8,128)S(1)} %get-tuple-element.164), kind=kOutput, calls=%fused_computation.10.clone.1 | convolution fusion | flops 467271680 | bytes 35667968 | tf_op jit(solution)/shard_map/while/body/eval_jaxpr/abhqk,abkhd->abqhd/dot_general | solution.py:89
  417.4 10.1 %fusion.124 = (bf16[2,4,1728,256]{3,2,1,0:T(8,128)(2,1)}, bf16[2,4,1728,256]{3,2,1,0:T(8,128)(2,1)}) fusion(bf16[2,4,1728,512]{3,2,1,0:T(8,128)(2,1)} %bitcast.268), kind=kLoop, calls=%fused_computation.105.clone.1 | loop fusion | bytes 28311552 | tf_op jit(solution)/shard_map/while/body/eval_jaxpr/slice | solution.py:78
  439.1 16.7 %fusion.126 = (f32[2,4,8,64]{3,2,1,0:T(8,128)S(1)}, f32[2,4,8,64,1728]{4,3,2,1,0:T(8,128)}) fusion(pred[2,4,1728]{2,1,0:T(4,128)(4,1)S(1)} %broadcast_in_dim.76, bf16[2,4,64,8,32]{2,4,3,1,0:T(8,128)(2,1)S(1)} %bitcast.276, bf16[2,4,1728,8,32]{2,4,3,1,0:T(8,128)(2,1)} %bitcast.269), kind=kOutput, calls=%fused_computation.106.clone.1 | convolution fusion | flops 481298112 | bytes 35681792 | tf_op jit(solution)/shard_map/while/body/eval_jaxpr/sub | solution.py:87
  465.8 13.6 %fusion.127 = bf16[2,4,8,32,64]{4,3,2,1,0:T(8,128)(2,1)S(1)} fusion(bf16[2,4,1728,8,32]{2,4,3,1,0:T(8,128)(2,1)} %bitcast.270, f32[2,4,8,64,1728]{4,3,2,1,0:T(8,128)} %get-tuple-element.163, f32[2,4,8,64]{3,2,1,0:T(8,128)S(1)} %get-tuple-element.164), kind=kOutput, calls=%fused_computation.10.clone.1 | convolution fusion | flops 467271680 | bytes 35667968 | tf_op jit(solution)/shard_map/while/body/eval_jaxpr/abhqk,abkhd->abqhd/dot_general | solution.py:89
  533.8 10.1 %fusion.124 = (bf16[2,4,1728,256]{3,2,1,0:T(8,128)(2,1)}, bf16[2,4,1728,256]{3,2,1,0:T(8,128)(2,1)}) fusion(bf16[2,4,1728,512]{3,2,1,0:T(8,128)(2,1)} %bitcast.268), kind=kLoop, calls=%fused_computation.105.clone.1 | loop fusion | bytes 28311552 | tf_op jit(solution)/shard_map/while/body/eval_jaxpr/slice | solution.py:78
  543.9 10.0 %copy.87 = bf16[2,4,1728,256]{2,3,1,0:T(8,128)(2,1)} copy(bf16[2,4,1728,256]{3,2,1,0:T(8,128)(2,1)} %get-tuple-element.162) | data formatting | bytes 14155776 | tf_op jit(solution)/shard_map/while/body/eval_jaxpr/slice | solution.py:78
  555.5 16.7 %fusion.126 = (f32[2,4,8,64]{3,2,1,0:T(8,128)S(1)}, f32[2,4,8,64,1728]{4,3,2,1,0:T(8,128)}) fusion(pred[2,4,1728]{2,1,0:T(4,128)(4,1)S(1)} %broadcast_in_dim.76, bf16[2,4,64,8,32]{2,4,3,1,0:T(8,128)(2,1)S(1)} %bitcast.276, bf16[2,4,1728,8,32]{2,4,3,1,0:T(8,128)(2,1)} %bitcast.269), kind=kOutput, calls=%fused_computation.106.clone.1 | convolution fusion | flops 481298112 | bytes 35681792 | tf_op jit(solution)/shard_map/while/body/eval_jaxpr/sub | solution.py:87
  582.1 13.6 %fusion.127 = bf16[2,4,8,32,64]{4,3,2,1,0:T(8,128)(2,1)S(1)} fusion(bf16[2,4,1728,8,32]{2,4,3,1,0:T(8,128)(2,1)} %bitcast.270, f32[2,4,8,64,1728]{4,3,2,1,0:T(8,128)} %get-tuple-element.163, f32[2,4,8,64]{3,2,1,0:T(8,128)S(1)} %get-tuple-element.164), kind=kOutput, calls=%fused_computation.10.clone.1 | convolution fusion | flops 467271680 | bytes 35667968 | tf_op jit(solution)/shard_map/while/body/eval_jaxpr/abhqk,abkhd->abqhd/dot_general | solution.py:89
  650.2 10.1 %fusion.124 = (bf16[2,4,1728,256]{3,2,1,0:T(8,128)(2,1)}, bf16[2,4,1728,256]{3,2,1,0:T(8,128)(2,1)}) fusion(bf16[2,4,1728,512]{3,2,1,0:T(8,128)(2,1)} %bitcast.268), kind=kLoop, calls=%fused_computation.105.clone.1 | loop fusion | bytes 28311552 | tf_op jit(solution)/shard_map/while/body/eval_jaxpr/slice | solution.py:78
  671.9 16.7 %fusion.126 = (f32[2,4,8,64]{3,2,1,0:T(8,128)S(1)}, f32[2,4,8,64,1728]{4,3,2,1,0:T(8,128)}) fusion(pred[2,4,1728]{2,1,0:T(4,128)(4,1)S(1)} %broadcast_in_dim.76, bf16[2,4,64,8,32]{2,4,3,1,0:T(8,128)(2,1)S(1)} %bitcast.276, bf16[2,4,1728,8,32]{2,4,3,1,0:T(8,128)(2,1)} %bitcast.269), kind=kOutput, calls=%fused_computation.106.clone.1 | convolution fusion | flops 481298112 | bytes 35681792 | tf_op jit(solution)/shard_map/while/body/eval_jaxpr/sub | solution.py:87
  698.5 13.6 %fusion.127 = bf16[2,4,8,32,64]{4,3,2,1,0:T(8,128)(2,1)S(1)} fusion(bf16[2,4,1728,8,32]{2,4,3,1,0:T(8,128)(2,1)} %bitcast.270, f32[2,4,8,64,1728]{4,3,2,1,0:T(8,128)} %get-tuple-element.163, f32[2,4,8,64]{3,2,1,0:T(8,128)S(1)} %get-tuple-element.164), kind=kOutput, calls=%fused_computation.10.clone.1 | convolution fusion | flops 467271680 | bytes 35667968 | tf_op jit(solution)/shard_map/while/body/eval_jaxpr/abhqk,abkhd->abqhd/dot_general | solution.py:89
  (215 shorter events, 313.7 us)
Async XLA Ops:
  0.0 87.7 %copy-start = (bf16[256,768]{1,0:T(8,128)(2,1)S(1)}, bf16[256,768]{1,0:T(8,128)(2,1)}, u32[]{:S(2)}) copy-start(bf16[256,768]{1,0:T(8,128)(2,1)} %param.13) | copy-start | bytes 1179652
  88.9 3.6 collective-permute-start
  90.2 4.6 collective-permute-start.1
  94.8 51.7 %copy-start.2 = (bf16[4,16,16,512]{3,2,1,0:T(8,128)(2,1)}, bf16[4,16,16,512]{3,2,1,0:T(8,128)(2,1)S(1)}, u32[]{:S(2)}) copy-start(bf16[4,16,16,512]{3,2,1,0:T(8,128)(2,1)S(1)} %collective-permute-done.1) | copy-start | bytes 3145732
  95.0 65.7 %copy-start.12 = (s32[27]{0:T(128)S(1)}, s32[27]{0:T(128)}, u32[]{:S(2)}) copy-start(s32[27]{0:T(128)} %constant.117) | copy-start | bytes 328
  95.1 65.8 %copy-start.11 = (s32[27]{0:T(128)S(1)}, s32[27]{0:T(128)}, u32[]{:S(2)}) copy-start(s32[27]{0:T(128)} %constant.119) | copy-start | bytes 328
  95.1 65.9 %copy-start.10 = (s32[27]{0:T(128)S(1)}, s32[27]{0:T(128)}, u32[]{:S(2)}) copy-start(s32[27]{0:T(128)} %constant.121) | copy-start | bytes 328
  95.1 65.9 %copy-start.7 = (s32[2,4,4]{2,1,0:T(4,128)S(1)}, s32[2,4,4]{2,1,0:T(4,128)}, u32[]{:S(2)}) copy-start(s32[2,4,4]{2,1,0:T(4,128)} %param.16) | copy-start | bytes 388
  95.1 65.9 %copy-start.9 = (s32[27]{0:T(128)S(1)}, s32[27]{0:T(128)}, u32[]{:S(2)}) copy-start(s32[27]{0:T(128)} %constant.122) | copy-start | bytes 328
  95.1 27.0 %collective-permute-start.2 = (bf16[16,4,16,512]{3,2,1,0:T(8,128)(2,1)S(1)}, bf16[16,4,16,512]{3,2,1,0:T(8,128)(2,1)S(1)}, u32[]{:S(2)}, u32[]{:S(2)}) collective-permute-start(bf16[16,4,16,512]{3,2,1,0:T(8,128)(2,1)S(1)} %get-tuple-element.116), channel_id=1, source_target_pairs={{0,4},{4,8},{8,12},{1,5},{5,9},{9,13},{2,6},{6,10},{10,14},{3,7},{... | collective-permute-start | bytes 3145736 | tf_op jit(solution)/shard_map/ppermute | solution.py:24
  99.5 47.0 %collective-permute-start.3 = (bf16[16,4,16,512]{3,2,1,0:T(8,128)(2,1)S(1)}, bf16[16,4,16,512]{3,2,1,0:T(8,128)(2,1)S(1)}, u32[]{:S(2)}, u32[]{:S(2)}) collective-permute-start(bf16[16,4,16,512]{3,2,1,0:T(8,128)(2,1)S(1)} %get-tuple-element.117), channel_id=1, source_target_pairs={{4,0},{8,4},{12,8},{5,1},{9,5},{13,9},{6,2},{10,6},{14,10},{7,3},{... | collective-permute-start | bytes 3145736 | tf_op jit(solution)/shard_map/ppermute | solution.py:26
  122.1 27.6 %copy-start.3 = (bf16[16,4,16,512]{3,2,1,0:T(8,128)(2,1)}, bf16[16,4,16,512]{3,2,1,0:T(8,128)(2,1)S(1)}, u32[]{:S(2)}) copy-start(bf16[16,4,16,512]{3,2,1,0:T(8,128)(2,1)S(1)} %collective-permute-done.2) | copy-start | bytes 3145732
  146.5 3.2 copy-start.4
  149.7 35.8 %collective-permute-start.4 = (bf16[16,24,4,512]{3,2,1,0:T(4,128)(2,1)}, bf16[16,24,4,512]{3,2,1,0:T(4,128)(2,1)}, u32[]{:S(2)}, u32[]{:S(2)}) collective-permute-start(bf16[16,24,4,512]{3,2,1,0:T(4,128)(2,1)} %get-tuple-element.114), channel_id=1, source_target_pairs={{0,1},{1,2},{2,3},{4,5},{5,6},{6,7},{8,9},{9,10},{10,11},{12,13},{... | collective-permute-start | bytes 4718600 | tf_op jit(solution)/shard_map/ppermute | solution.py:24
  153.3 37.5 %collective-permute-start.5 = (bf16[16,24,4,512]{3,2,1,0:T(4,128)(2,1)}, bf16[16,24,4,512]{3,2,1,0:T(4,128)(2,1)}, u32[]{:S(2)}, u32[]{:S(2)}) collective-permute-start(bf16[16,24,4,512]{3,2,1,0:T(4,128)(2,1)} %get-tuple-element.115), channel_id=1, source_target_pairs={{1,0},{2,1},{3,2},{5,4},{6,5},{7,6},{9,8},{10,9},{11,10},{13,12},{... | collective-permute-start | bytes 4718600 | tf_op jit(solution)/shard_map/ppermute | solution.py:26
  237.0 9.7 %copy-start.5 = (bf16[4,2,4,64,256]{4,2,3,1,0:T(4,128)(2,1)S(1)}, bf16[4,2,4,64,256]{4,2,3,1,0:T(4,128)(2,1)}, u32[]{:S(2)}) copy-start(bf16[4,2,4,64,256]{4,2,3,1,0:T(4,128)(2,1)} %custom-call.1) | copy-start | bytes 3145732
  246.7 466.7 %copy-start.6 = (bf16[256,256]{1,0:T(8,128)(2,1)S(1)}, bf16[256,256]{1,0:T(8,128)(2,1)}, u32[]{:S(2)}) copy-start(bf16[256,256]{1,0:T(8,128)(2,1)} %param.14) | copy-start | bytes 393220
  246.7 466.7 %copy-start.8 = (f32[256]{0:T(256)S(1)}, f32[256]{0:T(256)}, u32[]{:S(2)}) copy-start(f32[256]{0:T(256)} %param.15) | copy-start | bytes 3076
  712.5 2.4 copy-start.1
where the time goes:
time: 723 us; the launch traced here: 715 us
  local copies, waits for them, and re-layouts  387 us (54%)
  matrix products  124 us (17%)
  blocking collectives  82.2 us (11%)
  waiting for transfers between devices  78.5 us (11%)
  other arithmetic  19.3 us (3%)
  starting transfers between devices  13.3 us (2%)
  loops' own time  11 us (2%)
    while x104, local copies, waits for them, and re-layouts  196 us
    slice x8, local copies, waits for them, and re-layouts, attend_span(): keys = keyvals[..., :width].reshape(2, depth, 27 * 64, heads, head_dim)  80.3 us
    sub x4, matrix products, attend_span(): expd = jnp.exp(scores - top)  66.7 us
    dot_general x4, matrix products, attend_span(): jnp.einsum('abhqk,abkhd->abqhd', weights, values, preferred_element_type=...  54.4 us
    ppermute x3, waiting for transfers between devices, padded_2(): lax.ppermute(tail, axis, [(i, (i + 1) % count) for i in range(ends)])  46.5 us
    psum x1, blocking collectives, on_device(): mean = lax.psum(jnp.sum(grouped, axis=(0, 2)), ('gx', 'gy', 'gz')) / count  42 us
    psum x1, blocking collectives, on_device(): lax.psum(jnp.sum(centred * centred, axis=(0, 2)), ('gx', 'gy', 'gz'))  40.2 us
    slice x4, local copies, waits for them, and re-layouts, attend_span(): values = keyvals[..., width:].reshape(2, depth, 27 * 64, heads, head_dim)  39.9 us
  transfers between devices with their start and end apart: 6, of which 6 were waited for; matrix products, arithmetic and copies ran while one was open for 1% of the time, Pallas kernels for 0%

commit v1 on v0

v1 whole, which is shorter than its diff:
```python
import functools
import math

import jax
import jax.numpy as jnp
from jax import lax
from jax.experimental import pallas as pl
from jax.experimental.pallas import tpu as pltpu
from jax.sharding import PartitionSpec as P

HEADS = 8
GROUPS = 32
CELLS = 64
CHUNK = 4
LOW = -1e30


def halo(blocks, sides):
    for axis, dim in sides:
        count = lax.axis_size(axis)
        ends = count - 1
        head = lax.slice_in_dim(blocks, 0, 1, axis=dim)
        tail = lax.slice_in_dim(blocks, blocks.shape[dim] - 1, blocks.shape[dim], axis=dim)
        blocks = jnp.concatenate(
            [
                lax.ppermute(tail, axis, [(i, i + 1) for i in range(ends)]),
                blocks,
                lax.ppermute(head, axis, [(i + 1, i) for i in range(ends)]),
            ],
            axis=dim,
        )
    return blocks


def to_blocks(field):
    size_x, size_y, size_z, chans = field.shape
    shaped = field.reshape(size_x // 4, 4, size_y // 4, 4, size_z // 4, 4, chans)
    return shaped.transpose(0, 2, 4, 1, 3, 5, 6).reshape(
        size_x // 4, size_y // 4, size_z // 4, CELLS, chans
    )


def attend_kernel(
    counts, place_ref, limit_ref, x_ref, mean_ref, gain_ref, shift_ref, wqkv_ref, wout_ref,
    bout_ref, out_ref, k_ref, v_ref, s_ref, top_ref, sum_ref, acc_ref, mix_ref,
):
    count_x, count_y, count_z = counts
    pad_y, pad_z = count_y + 2, count_z + 2
    width = x_ref.shape[1]
    head_dim = width // HEADS
    rows = HEADS * CELLS
    keys = CHUNK * CELLS
    factor = head_dim ** (-0.5) * math.log2(math.e)

    def normed(x):
        scaled = (x.astype(jnp.float32) - mean_ref[...]) * gain_ref[...]
        return (scaled + shift_ref[...]).astype(jnp.bfloat16)

    def low(axis, index):
        return jnp.where(place_ref[axis] + index > 0, index, index + 1)

    def high(axis, index):
        return jnp.where(place_ref[axis] + index + 1 < place_ref[3 + axis], index + 2, index + 1)

    first_x, last_x = low(0, 0), high(0, count_x - 1)
    first_y, last_y = low(1, 0), high(1, count_y - 1)
    column = pad_z * CELLS

    def project(index, carry):
        index_x, index_y = index // pad_y, index % pad_y
        inside = (
            (index_x >= first_x) & (index_x <= last_x) & (index_y >= first_y) & (index_y <= last_y)
        )

        @pl.when(inside)
        def _():
            span = pl.ds(pl.multiple_of(index * column, column), column)
            cells = normed(x_ref[span, :])
            k_ref[span, :] = jnp.dot(
                cells, wqkv_ref[:, width : 2 * width], preferred_element_type=jnp.float32
            ).astype(jnp.bfloat16)
            v_ref[span, :] = jnp.dot(
                cells, wqkv_ref[:, 2 * width :], preferred_element_type=jnp.float32
            ).astype(jnp.bfloat16)

        return carry

    lax.fori_loop(0, (count_x + 2) * pad_y, project, 0)

    lane_head = lax.broadcasted_iota(jnp.int32, (CELLS, width), 1) // head_dim

    def one_block(block_x, block_y, block_z):
        limit = limit_ref[(block_x * count_y + block_y) * count_z + block_z]
        lo_x, hi_x = low(0, block_x), high(0, block_x)
        lo_y, hi_y = low(1, block_y), high(1, block_y)
        lo_z = jnp.where(limit > 0, low(2, block_z), block_z + 1)
        hi_z = jnp.where(limit > 0, high(2, block_z), block_z + 1)
        total = (hi_x - lo_x + 1) * (hi_y - lo_y + 1) * (hi_z - lo_z + 1)
        full = total // CHUNK
        chunks = (total + CHUNK - 1) // CHUNK
        start = (lo_x, lo_y, lo_z)

        def flat(at_x, at_y, at_z):
            return (at_x * pad_y + at_y) * pad_z + at_z

        def gather(ref, at):
            pieces = []
            at_x, at_y, at_z = at
            for _ in range(CHUNK):
                index = pl.multiple_of(flat(at_x, at_y, at_z) * CELLS, CELLS)
                pieces.append(ref[pl.ds(index, CELLS), :])
                turn_z = at_z == hi_z
                at_z = jnp.where(turn_z, lo_z, at_z + 1)
                turn_y = turn_z & (at_y == hi_y)
                at_y = jnp.where(turn_y, lo_y, jnp.where(turn_z, at_y + 1, at_y))
                at_x = jnp.where(turn_y, jnp.minimum(at_x + 1, hi_x), at_x)
            return jnp.concatenate(pieces, axis=0), (at_x, at_y, at_z)

        own = pl.multiple_of(flat(block_x + 1, block_y + 1, block_z + 1) * CELLS, CELLS)
        query = jnp.dot(
            normed(x_ref[pl.ds(own, CELLS), :]),
            wqkv_ref[:, :width],
            preferred_element_type=jnp.float32,
        )
        stacked = jnp.concatenate(
            [jnp.where(lane_head == head, query, 0.0).astype(jnp.bfloat16) for head in range(HEADS)],
            axis=0,
        )
        top_ref[...] = jnp.full_like(top_ref, LOW)

        def score(index, at, masked):
            chunk, at = gather(k_ref, at)
            scores = lax.dot_general(
                stacked, chunk, (((1,), (1,)), ((), ())), preferred_element_type=jnp.float32
            )
            if masked:
                lane = lax.broadcasted_iota(jnp.int32, (1, keys), 1) + index * keys
                scores = jnp.where(lane < total * CELLS, scores, LOW)
            s_ref[index] = scores
            best = scores[:, :128]
            for part in range(1, keys // 128):
                best = jnp.maximum(best, scores[:, part * 128 : (part + 1) * 128])
            top_ref[...] = jnp.maximum(top_ref[...], best)
            return at

        at = lax.fori_loop(0, full, functools.partial(score, masked=False), start)

        @pl.when(chunks > full)
        def _():
            score(full, at, True)

        top = jnp.max(top_ref[...], axis=1, keepdims=True) * factor
        top_ref[...] = jnp.broadcast_to(top, top_ref.shape)
        sum_ref[...] = jnp.zeros_like(sum_ref)
        acc_ref[...] = jnp.zeros_like(acc_ref)

        def mix(index, at):
            chunk, at = gather(v_ref, at)
            weights = []
            added = None
            for part in range(keys // 128):
                scores = s_ref[index, :, part * 128 : (part + 1) * 128]
                weight = jnp.exp2(scores * factor - top_ref[...])
                added = weight if added is None else added + weight
                weights.append(weight.astype(jnp.bfloat16))
            sum_ref[...] += added
            acc_ref[...] += jnp.dot(
                jnp.concatenate(weights, axis=1), chunk, preferred_element_type=jnp.float32
            )
            return at

        lax.fori_loop(0, chunks, mix, start)
        share = 1.0 / jnp.sum(sum_ref[...], axis=1, keepdims=True)
        mixed = jnp.zeros((CELLS, width), jnp.float32)
        for head in range(HEADS):
            part = slice(head * CELLS, (head + 1) * CELLS)
            mixed = jnp.where(lane_head == head, acc_ref[part, :] * share[part], mixed)
        return mixed.astype(jnp.bfloat16)

    slab = count_z * CELLS
    natural = lax.broadcasted_iota(jnp.int32, (slab, slab), 0)
    blocked = lax.broadcasted_iota(jnp.int32, (slab, slab), 1)
    depth = natural % (count_z * 4)
    moved = depth // 4 * CELLS + natural // (count_z * 4) * 4 + depth % 4
    order = (moved == blocked).astype(jnp.bfloat16)

    def one_column(index, carry):
        block_x, block_y = index // count_y, index % count_y

        def one_depth(block_z, carry):
            span = pl.ds(pl.multiple_of(block_z * CELLS, CELLS), CELLS)
            mix_ref[span, :] = one_block(block_x, block_y, block_z)
            return carry

        lax.fori_loop(0, count_z, one_depth, 0)
        cells = jnp.dot(order, mix_ref[...], preferred_element_type=jnp.float32)
        result = jnp.dot(
            cells.astype(jnp.bfloat16), wout_ref[...], preferred_element_type=jnp.float32
        )
        result = (result + bout_ref[...]).astype(jnp.bfloat16)
        out_ref[pl.ds(block_x * 4, 4), pl.ds(block_y * 4, 4), :, :] = result.reshape(
            4, 4, count_z * 4, width
        )
        return carry

    lax.fori_loop(0, count_x * count_y, one_column, 0)


def attend(place, limit, padded, mean, gain, shift, w_qkv, w_out, b_out):
    counts = limit.shape
    width = padded.shape[-1]
    flat = padded.reshape(-1, width)
    rows = HEADS * CELLS
    most = -(-27 // CHUNK)
    smem = pl.BlockSpec(memory_space=pltpu.SMEM)
    vmem = pl.BlockSpec(memory_space=pltpu.VMEM)
    return pl.pallas_call(
        functools.partial(attend_kernel, counts),
        out_shape=jax.ShapeDtypeStruct(
            (counts[0] * 4, counts[1] * 4, counts[2] * 4, width), jnp.bfloat16
        ),
        in_specs=[smem, smem] + [vmem] * 7,
        out_specs=vmem,
        scratch_shapes=[
            pltpu.VMEM(flat.shape, jnp.bfloat16),
            pltpu.VMEM(flat.shape, jnp.bfloat16),
            pltpu.VMEM((most, rows, CHUNK * CELLS), jnp.float32),
            pltpu.VMEM((rows, 128), jnp.float32),
            pltpu.VMEM((rows, 128), jnp.float32),
            pltpu.VMEM((rows, width), jnp.float32),
            pltpu.VMEM((counts[2] * CELLS, width), jnp.bfloat16),
        ],
        compiler_params=pltpu.CompilerParams(vmem_limit_bytes=48 * 2**20),
        cost_estimate=pl.CostEstimate(
            flops=30 * 10**9, bytes_accessed=7 * 10**6, transcendentals=28 * 10**6
        ),
    )(place, limit.reshape(-1), flat, mean, gain, shift, w_qkv, w_out, b_out)


def on_device(latent, norm_gain, norm_shift, w_qkv, w_out, b_out, depth_limit):
    width = latent.shape[-1]
    per = width // GROUPS
    axes = ("gx", "gy", "gz")
    grouped = latent.astype(jnp.float32).reshape(-1, GROUPS, per)
    count = grouped.shape[0] * per
    mean_here = jnp.sum(grouped, axis=(0, 2)) / count
    centred = grouped - mean_here[None, :, None]
    square_here = jnp.sum(centred * centred, axis=(0, 2)) / count
    parts = lax.all_gather(jnp.stack([mean_here, square_here]), axes)
    mean = jnp.mean(parts[:, 0], axis=0)
    var = jnp.mean(parts[:, 1] + (parts[:, 0] - mean) ** 2, axis=0)
    gain = jnp.repeat(lax.rsqrt(var + 1e-06), per) * norm_gain
    padded = halo(to_blocks(latent), (("gy", 1), ("gz", 2), ("gx", 0)))
    counts = depth_limit.shape
    place = jnp.stack(
        [lax.axis_index(axis) * n for axis, n in zip(axes, counts)]
        + [jnp.int32(lax.axis_size(axis) * n) for axis, n in zip(axes, counts)]
    ).astype(jnp.int32)
    return attend(
        place, depth_limit, padded, jnp.repeat(mean, per)[None], gain[None], norm_shift[None],
        w_qkv, w_out, b_out[None],
    )


def solution(mesh):
    placed = (P("gx", "gy", "gz", None), P(), P(), P(), P(), P(), P("gx", "gy", "gz"))
    return jax.shard_map(
        on_device, mesh=mesh, in_specs=placed, out_specs=P("gx", "gy", "gz", None), check_vma=False
    )
```

time: 723 us -> 212 us (0.29)
  the two profiles are of different devices: /device:TPU:0 before, /device:TPU:20 now
where the time goes in v1:
time: 212 us; the launch traced here: 211 us
  Pallas kernels  98.4 us (46%)
  blocking collectives  70.2 us (33%)
  starting transfers between devices  16.1 us (8%)
  waiting for transfers between devices  15.1 us (7%)
  local copies, waits for them, and re-layouts  7.13 us (3%)
  other arithmetic  4 us (2%)
    pallas_call x1, Pallas kernels, attend(): pl.pallas_call(functools.partial(attend_kernel, counts), out_shape=jax.Sh...  98.4 us
    all_gather x1, blocking collectives, on_device(): parts = lax.all_gather(jnp.stack([mean_here, square_here]), axes)  70.2 us
    ppermute x3, waiting for transfers between devices, halo(): lax.ppermute(tail, axis, [(i, i + 1) for i in range(ends)])  10.8 us
    ppermute x3, starting transfers between devices, halo(): lax.ppermute(tail, axis, [(i, i + 1) for i in range(ends)])  9.17 us
    ppermute x3, starting transfers between devices, halo(): lax.ppermute(head, axis, [(i + 1, i) for i in range(ends)])  6.98 us
    ppermute x3, waiting for transfers between devices, halo(): lax.ppermute(head, axis, [(i + 1, i) for i in range(ends)])  4.37 us
  transfers between devices with their start and end apart: 6, of which 4 were waited for; matrix products, arithmetic and copies ran while one was open for 2% of the time, Pallas kernels for 0%

profile of v1, /device:TPU:20, one launch (start us, length us, event | category | flops | bytes accessed | tf_op | source)
XLA Modules:
  0.0 211.2 jit_solution(9084118302211904289)
XLA Ops:
  0.0 1.3 reshape.44
  1.4 0.6 copy.12
  1.9 0.3 reshape.45
  2.3 3.4 %collective-permute-start = (bf16[2,1,4,64,256]{4,3,2,1,0:T(8,128)(2,1)S(1)}, bf16[2,1,4,64,256]{4,3,2,1,0:T(8,128)(2,1)S(1)}, u32[]{:S(2)}, u32[]{:S(2)}) collective-permute-start(bf16[2,1,4,64,256]{4,3,2,1,0:T(8,128)(2,1)S(1)} %get-tuple-element.10), channel_id=1, source_target_pairs={{0,4},{4,8},{8,12},{1,5},{5,9},{9,13},{2,6},{6,10},{10,14},{3,7},{... | collective-permute-start | bytes 786440 | tf_op jit(solution)/shard_map/ppermute | solution.py:26
  5.7 3.3 %collective-permute-start.1 = (bf16[2,1,4,64,256]{4,3,2,1,0:T(8,128)(2,1)S(1)}, bf16[2,1,4,64,256]{4,3,2,1,0:T(8,128)(2,1)S(1)}, u32[]{:S(2)}, u32[]{:S(2)}) collective-permute-start(bf16[2,1,4,64,256]{4,3,2,1,0:T(8,128)(2,1)S(1)} %get-tuple-element.9), channel_id=1, source_target_pairs={{4,0},{8,4},{12,8},{5,1},{9,5},{13,9},{6,2},{10,6},{14,10},{7,3},{... | collective-permute-start | bytes 786440 | tf_op jit(solution)/shard_map/ppermute | solution.py:28
  9.0 5.2 %collective-permute-done = bf16[2,1,4,64,256]{4,3,2,1,0:T(8,128)(2,1)S(1)} collective-permute-done((bf16[2,1,4,64,256]{4,3,2,1,0:T(8,128)(2,1)S(1)}, bf16[2,1,4,64,256]{4,3,2,1,0:T(8,128)(2,1)S(1)}, u32[]{:S(2)}, u32[]{:S(2)}) %collective-permute-start) | collective-permute-done | bytes 262176 | tf_op jit(solution)/shard_map/ppermute | solution.py:26
  14.3 1.4 constant_dynamic-update-slice_fusion.1
  15.7 1.2 collective-permute-done.1
  16.9 0.9 fusion.4
  17.8 3.5 %collective-permute-start.2 = (bf16[2,6,1,64,256]{4,3,2,1,0:T(8,128)(2,1)}, bf16[2,6,1,64,256]{4,3,2,1,0:T(8,128)(2,1)S(1)}, u32[]{:S(2)}, u32[]{:S(2)}) collective-permute-start(bf16[2,6,1,64,256]{4,3,2,1,0:T(8,128)(2,1)} %get-tuple-element.7), channel_id=1, source_target_pairs={{0,1},{1,2},{2,3},{4,5},{5,6},{6,7},{8,9},{9,10},{10,11},{12,13},{... | collective-permute-start | bytes 1179656 | tf_op jit(solution)/shard_map/ppermute | solution.py:26
  21.3 2.4 %collective-permute-start.3 = (bf16[2,6,1,64,256]{4,3,2,1,0:T(8,128)(2,1)}, bf16[2,6,1,64,256]{4,3,2,1,0:T(8,128)(2,1)S(1)}, u32[]{:S(2)}, u32[]{:S(2)}) collective-permute-start(bf16[2,6,1,64,256]{4,3,2,1,0:T(8,128)(2,1)} %get-tuple-element.8), channel_id=1, source_target_pairs={{1,0},{2,1},{3,2},{5,4},{6,5},{7,6},{9,8},{10,9},{11,10},{13,12},{... | collective-permute-start | bytes 1179656 | tf_op jit(solution)/shard_map/ppermute | solution.py:28
  23.6 0.3 convert_reduce_fusion
  24.0 0.1 reduce_sum.52
  24.3 5.5 %collective-permute-done.2 = bf16[2,6,1,64,256]{4,3,2,1,0:T(8,128)(2,1)S(1)} collective-permute-done((bf16[2,6,1,64,256]{4,3,2,1,0:T(8,128)(2,1)}, bf16[2,6,1,64,256]{4,3,2,1,0:T(8,128)(2,1)S(1)}, u32[]{:S(2)}, u32[]{:S(2)}) %collective-permute-start.2) | collective-permute-done | bytes 393248 | tf_op jit(solution)/shard_map/ppermute | solution.py:26
  29.9 3.2 %collective-permute-done.3 = bf16[2,6,1,64,256]{4,3,2,1,0:T(8,128)(2,1)S(1)} collective-permute-done((bf16[2,6,1,64,256]{4,3,2,1,0:T(8,128)(2,1)}, bf16[2,6,1,64,256]{4,3,2,1,0:T(8,128)(2,1)S(1)}, u32[]{:S(2)}, u32[]{:S(2)}) %collective-permute-start.3) | collective-permute-done | bytes 393248 | tf_op jit(solution)/shard_map/ppermute | solution.py:28
  33.1 0.3 pad_maximum_fusion.1
  33.4 1.7 fusion.3
  35.1 2.3 %collective-permute-start.4 = (bf16[1,6,6,64,256]{4,3,2,1,0:T(8,128)(2,1)}, bf16[1,6,6,64,256]{4,3,2,1,0:T(8,128)(2,1)}, u32[]{:S(2)}, u32[]{:S(2)}) collective-permute-start(bf16[1,6,6,64,256]{4,3,2,1,0:T(8,128)(2,1)} %get-tuple-element.5), channel_id=1, source_target_pairs={{0,16},{1,17},{2,18},{3,19},{4,20},{5,21},{6,22},{7,23},{8,24},{9,... | collective-permute-start | bytes 3538952 | tf_op jit(solution)/shard_map/ppermute | solution.py:26
  37.4 1.3 collective-permute-start.5
  38.7 0.3 fusion.1
  39.1 0.1 reduce_sum.55
  39.2 70.2 %all-gather.1 = f32[32,2,32]{2,1,0:T(2,128)S(1)} all-gather(f32[1,2,32]{2,1,0:T(2,128)S(1)} %maximum_bitcast_fusion), channel_id=2, replica_groups=mesh['gx'=2,'gy'=4,'gz'=4] {'gx','gy','gz'}, dimensions={0}, use_global_device_ids=true | all-gather | bytes 8448 | tf_op jit(solution)/shard_map/all_gather | solution.py:249
  110.1 2.7 %pad_maximum_fusion = bf16[4,6,6,64,256]{4,3,2,1,0:T(8,128)(2,1)S(1)} fusion(bf16[1,6,6,64,256]{4,3,2,1,0:T(8,128)(2,1)} %collective-permute-done.5, bf16[2,6,1,64,256]{4,3,2,1,0:T(8,128)(2,1)S(1)} %collective-permute-done.3, bf16[2,6,4,64,256]{4,3,2,1,0:T(8,128)(2,1)S(1)} %constant_dynamic-update-slice_fusion, ...), kind=kLoop, calls=%fused_computation | loop fusion | flops 9437184 | bytes 9437184 | tf_op jit(solution)/shard_map/concatenate | solution.py:24
  112.9 98.4 %shard_map.73 = bf16[8,16,16,256]{3,2,1,0:T(8,128)(2,1)} custom-call(s32[6]{0:T(128)S(1)} %stack.20.place_ref, s32[32]{0:T(128)S(1)} %reshape.43.limit_ref, bf16[9216,256]{1,0:T(8,128)(2,1)S(1)} %bitcast.20, f32[1,256]{1,0:T(1,128)S(1)} %broadcast_in_dim_reshape.3.mean_ref, f32[1,256]{1,0:T(1,128)S(1)} %bitcast.21, f32[1,256]{1,0:T(1,128)S(1)} %bitcast.22, ...), custom_call_target="tpu_custom_call" | custom-call | flops 30000001024 | bytes 7000000 | tf_op jit(solution)/shard_map/pallas_call | solution.py:217
  (40 shorter events, 1.1 us)
Async XLA Ops:
  2.2 6.8 %copy-start.5 = (bf16[2,4,4,64,256]{4,3,2,1,0:T(8,128)(2,1)}, bf16[2,4,4,64,256]{4,3,2,1,0:T(8,128)(2,1)S(1)}, u32[]{:S(2)}) copy-start(bf16[2,4,4,64,256]{4,3,2,1,0:T(8,128)(2,1)S(1)} %reshape.45) | copy-start | bytes 3145732
  2.3 12.0 %collective-permute-start = (bf16[2,1,4,64,256]{4,3,2,1,0:T(8,128)(2,1)S(1)}, bf16[2,1,4,64,256]{4,3,2,1,0:T(8,128)(2,1)S(1)}, u32[]{:S(2)}, u32[]{:S(2)}) collective-permute-start(bf16[2,1,4,64,256]{4,3,2,1,0:T(8,128)(2,1)S(1)} %get-tuple-element.10), channel_id=1, source_target_pairs={{0,4},{4,8},{8,12},{1,5},{5,9},{9,13},{2,6},{6,10},{10,14},{3,7},{... | collective-permute-start | bytes 786440 | tf_op jit(solution)/shard_map/ppermute | solution.py:26
  5.7 11.2 %collective-permute-start.1 = (bf16[2,1,4,64,256]{4,3,2,1,0:T(8,128)(2,1)S(1)}, bf16[2,1,4,64,256]{4,3,2,1,0:T(8,128)(2,1)S(1)}, u32[]{:S(2)}, u32[]{:S(2)}) collective-permute-start(bf16[2,1,4,64,256]{4,3,2,1,0:T(8,128)(2,1)S(1)} %get-tuple-element.9), channel_id=1, source_target_pairs={{4,0},{8,4},{12,8},{5,1},{9,5},{13,9},{6,2},{10,6},{14,10},{7,3},{... | collective-permute-start | bytes 786440 | tf_op jit(solution)/shard_map/ppermute | solution.py:28
  14.3 9.4 %copy-start.4 = (bf16[8,16,16,256]{3,2,1,0:T(8,128)(2,1)S(1)}, bf16[8,16,16,256]{3,2,1,0:T(8,128)(2,1)}, u32[]{:S(2)}) copy-start(bf16[8,16,16,256]{3,2,1,0:T(8,128)(2,1)} %param.7) | copy-start | bytes 3145732
  17.8 12.1 %collective-permute-start.2 = (bf16[2,6,1,64,256]{4,3,2,1,0:T(8,128)(2,1)}, bf16[2,6,1,64,256]{4,3,2,1,0:T(8,128)(2,1)S(1)}, u32[]{:S(2)}, u32[]{:S(2)}) collective-permute-start(bf16[2,6,1,64,256]{4,3,2,1,0:T(8,128)(2,1)} %get-tuple-element.7), channel_id=1, source_target_pairs={{0,1},{1,2},{2,3},{4,5},{5,6},{6,7},{8,9},{9,10},{10,11},{12,13},{... | collective-permute-start | bytes 1179656 | tf_op jit(solution)/shard_map/ppermute | solution.py:26
  21.3 11.8 %collective-permute-start.3 = (bf16[2,6,1,64,256]{4,3,2,1,0:T(8,128)(2,1)}, bf16[2,6,1,64,256]{4,3,2,1,0:T(8,128)(2,1)S(1)}, u32[]{:S(2)}, u32[]{:S(2)}) collective-permute-start(bf16[2,6,1,64,256]{4,3,2,1,0:T(8,128)(2,1)} %get-tuple-element.8), channel_id=1, source_target_pairs={{1,0},{2,1},{3,2},{5,4},{6,5},{7,6},{9,8},{10,9},{11,10},{13,12},{... | collective-permute-start | bytes 1179656 | tf_op jit(solution)/shard_map/ppermute | solution.py:28
  33.4 76.5 %copy-start.6 = (s32[2,4,4]{2,1,0:T(4,128)S(1)}, s32[2,4,4]{2,1,0:T(4,128)}, u32[]{:S(2)}) copy-start(s32[2,4,4]{2,1,0:T(4,128)} %param.13) | copy-start | bytes 388
  33.4 76.5 %copy-start.7 = (f32[256]{0:T(256)S(1)}, f32[256]{0:T(256)}, u32[]{:S(2)}) copy-start(f32[256]{0:T(256)} %param.8) | copy-start | bytes 3076
  35.1 75.0 %collective-permute-start.4 = (bf16[1,6,6,64,256]{4,3,2,1,0:T(8,128)(2,1)}, bf16[1,6,6,64,256]{4,3,2,1,0:T(8,128)(2,1)}, u32[]{:S(2)}, u32[]{:S(2)}) collective-permute-start(bf16[1,6,6,64,256]{4,3,2,1,0:T(8,128)(2,1)} %get-tuple-element.5), channel_id=1, source_target_pairs={{0,16},{1,17},{2,18},{3,19},{4,20},{5,21},{6,22},{7,23},{8,24},{9,... | collective-permute-start | bytes 3538952 | tf_op jit(solution)/shard_map/ppermute | solution.py:26
  37.4 72.7 %collective-permute-start.5 = (bf16[1,6,6,64,256]{4,3,2,1,0:T(8,128)(2,1)}, bf16[1,6,6,64,256]{4,3,2,1,0:T(8,128)(2,1)}, u32[]{:S(2)}, u32[]{:S(2)}) collective-permute-start(bf16[1,6,6,64,256]{4,3,2,1,0:T(8,128)(2,1)} %get-tuple-element.6), channel_id=1, source_target_pairs={{16,0},{17,1},{18,2},{19,3},{20,4},{21,5},{22,6},{23,7},{24,8},{25... | collective-permute-start | bytes 3538952 | tf_op jit(solution)/shard_map/ppermute | solution.py:28
  110.0 2.8 %copy-start = (bf16[256,768]{1,0:T(8,128)(2,1)S(1)}, bf16[256,768]{1,0:T(8,128)(2,1)}, u32[]{:S(2)}) copy-start(bf16[256,768]{1,0:T(8,128)(2,1)} %wqkv_ref.1) | copy-start | bytes 1179652
  110.0 2.8 %copy-start.1 = (bf16[256,256]{1,0:T(8,128)(2,1)S(1)}, bf16[256,256]{1,0:T(8,128)(2,1)}, u32[]{:S(2)}) copy-start(bf16[256,256]{1,0:T(8,128)(2,1)} %wout_ref.1) | copy-start | bytes 393220
  110.0 2.8 %copy-start.2 = (f32[256]{0:T(256)S(1)}, f32[256]{0:T(256)}, u32[]{:S(2)}) copy-start(f32[256]{0:T(256)} %param.9) | copy-start | bytes 3076
  110.0 2.8 %copy-start.3 = (f32[256]{0:T(256)S(1)}, f32[256]{0:T(256)}, u32[]{:S(2)}) copy-start(f32[256]{0:T(256)} %param.12) | copy-start | bytes 3076

commit v2 on v1

--- a/solution.py
+++ b/solution.py
@@ -15,34 +15,211 @@
 LOW = -1e30
 
 
-def halo(blocks, sides):
-    for axis, dim in sides:
-        count = lax.axis_size(axis)
-        ends = count - 1
-        head = lax.slice_in_dim(blocks, 0, 1, axis=dim)
-        tail = lax.slice_in_dim(blocks, blocks.shape[dim] - 1, blocks.shape[dim], axis=dim)
-        blocks = jnp.concatenate(
-            [
-                lax.ppermute(tail, axis, [(i, i + 1) for i in range(ends)]),
-                blocks,
-                lax.ppermute(head, axis, [(i + 1, i) for i in range(ends)]),
-            ],
-            axis=dim,
-        )
-    return blocks
-
-
-def to_blocks(field):
-    size_x, size_y, size_z, chans = field.shape
-    shaped = field.reshape(size_x // 4, 4, size_y // 4, 4, size_z // 4, 4, chans)
-    return shaped.transpose(0, 2, 4, 1, 3, 5, 6).reshape(
-        size_x // 4, size_y // 4, size_z // 4, CELLS, chans
-    )
+def cell_order(slab, inverse):
+    natural = lax.broadcasted_iota(jnp.int32, (slab, slab), 0 if inverse else 1)
+    blocked = lax.broadcasted_iota(jnp.int32, (slab, slab), 1 if inverse else 0)
+    depth = blocked // CELLS * 4 + blocked % 4
+    found = blocked % CELLS // 4 * (slab // 16) + depth
+    return (found == natural).astype(jnp.bfloat16)
+
+
+def exchange_kernel(counts, sizes, latent_ref, pad_ref, stats_ref, here, there, *sems):
+    send_sem, recv_sem, stat_send, stat_recv = sems
+    count_x, count_y, count_z = counts
+    width = latent_ref.shape[-1]
+    slab = count_z * CELLS
+    axes = ("gx", "gy", "gz")
+    me = [lax.axis_index(axis) for axis in axes]
+
+    def at(axis, position):
+        return tuple(position if n == axis else me[n] for n in range(3))
+
+    barrier = pltpu.get_barrier_semaphore()
+    for axis in range(3):
+        for step in range(1, sizes[axis]):
+            pl.semaphore_signal(
+                barrier, inc=1, device_id=at(axis, lax.rem(me[axis] + step, sizes[axis])),
+                device_id_type=pl.DeviceIdType.MESH,
+            )
+
+    order = cell_order(slab, False)
+    for block_x in range(count_x):
+        for block_y in range(count_y):
+            cells = latent_ref[
+                block_x * 4 : block_x * 4 + 4, block_y * 4 : block_y * 4 + 4, :, :
+            ].reshape(slab, width)
+            blocks = jnp.dot(order, cells, preferred_element_type=jnp.float32)
+            pad_ref[1 + block_x, 1 + block_y, 1 : 1 + count_z] = (
+                blocks.astype(jnp.bfloat16).reshape(count_z, CELLS, width)
+            )
+    pl.semaphore_wait(barrier, sum(sizes) - 3)
+
+    def has(axis, step):
+        return me[axis] > 0 if step < 0 else me[axis] < sizes[axis] - 1
+
+    copies = []
+
+    def layer(axis, side, spans):
+        count = counts[axis]
+        source = list(spans)
+        target = list(spans)
+        source[axis] = pl.ds(1 if side < 0 else count, 1)
+        target[axis] = pl.ds(count + 1 if side < 0 else 0, 1)
+        return tuple(source), tuple(target)
+
+    def send(axis, side, spans, given=None):
+        number = len(copies)
+        source, target = layer(axis, side, spans)
+        to = me[axis] + side
+        copy = pltpu.make_async_remote_copy(
+            src_ref=pad_ref.at[source],
+            dst_ref=pad_ref.at[target],
+            send_sem=send_sem.at[number],
+            recv_sem=recv_sem.at[number],
+            device_id=at(axis, to),
+            device_id_type=pl.DeviceIdType.MESH,
+        )
+        leaves, comes = has(axis, side), has(axis, -side)
+        if given is not None:
+            leaves, comes = leaves & given, comes & given
+        copies.append((copy, leaves, comes))
+
+        @pl.when(leaves)
+        def _():
+            copy.start()
+
+        return number
+
+    def received(number):
+        copy, _, comes = copies[number]
+
+        @pl.when(comes)
+        def _():
+            copy.wait_recv()
+
+    inner = [pl.ds(1, count) for count in counts]
+    sides = (-1, 1)
+    face_y = [send(1, side, inner) for side in sides]
+    face_z = [send(2, side, inner) for side in sides]
+    face_x = [send(0, side, inner) for side in sides]
+
+    cells = latent_ref[...].reshape(-1, width).astype(jnp.float32)
+    count = cells.shape[0]
+    mean = jnp.sum(cells, axis=0, keepdims=True) / count
+    centred = cells - mean
+    var = jnp.sum(centred * centred, axis=0, keepdims=True) / count
+
+    first = {0: 0, 1: sizes[0] - 1, 2: sizes[0] + sizes[1] - 2}
+
+    def stat_copies(axis):
+        found = []
+        for step in range(1, sizes[axis]):
+            slot = first[axis] + step - 1
+            found.append(
+                pltpu.make_async_remote_copy(
+                    src_ref=here.at[axis],
+                    dst_ref=there.at[slot],
+                    send_sem=stat_send.at[slot],
+                    recv_sem=stat_recv.at[slot],
+                    device_id=at(axis, lax.rem(me[axis] + step, sizes[axis])),
+                    device_id_type=pl.DeviceIdType.MESH,
+                )
+            )
+        return found
+
+    def stat_start(axis, mean, var):
+        here[axis, 0:1, :] = mean
+        here[axis, 1:2, :] = var
+        found = stat_copies(axis)
+        for copy in found:
+            copy.start()
+        return found
+
+    def stat_end(axis, found, mean, var):
+        for copy in found:
+            copy.wait()
+        means, variances = [mean], [var]
+        for step in range(1, sizes[axis]):
+            slot = first[axis] + step - 1
+            means.append(there[slot, 0:1, :])
+            variances.append(there[slot, 1:2, :])
+        mean = sum(means) / sizes[axis]
+        spread = [(part - mean) * (part - mean) for part in means]
+        return mean, (sum(variances) + sum(spread)) / sizes[axis]
+
+    found = stat_start(0, mean, var)
+    mean, var = stat_end(0, found, mean, var)
+    found = stat_start(1, mean, var)
+
+    outer_y = [pl.ds(0, 1), pl.ds(count_y + 1, 1)]
+    edge_z = []
+    for number, side in enumerate(sides):
+        received(face_y[1 - number])
+        spans = [inner[0], outer_y[number], inner[2]]
+        edge_z += [send(2, way, spans, has(1, side)) for way in sides]
+    mean, var = stat_end(1, found, mean, var)
+    found = stat_start(2, mean, var)
+    for number, side in enumerate(sides):
+        spans = [inner[0], outer_y[number], inner[2]]
+        face_x += [send(0, way, spans, has(1, side)) for way in sides]
+    mean, var = stat_end(2, found, mean, var)
+    stats_ref[...] = jnp.zeros_like(stats_ref)
+    stats_ref[0:1, :] = mean
+    stats_ref[1:2, :] = var
+    outer_z = [pl.ds(0, 1), pl.ds(count_z + 1, 1)]
+    for number, side in enumerate(sides):
+        received(face_z[1 - number])
+        spans = [inner[0], inner[1], outer_z[number]]
+        face_x += [send(0, way, spans, has(2, side)) for way in sides]
+    for number, side in enumerate(sides):
+        for other, side_y in enumerate(sides):
+            received(edge_z[other * 2 + 1 - number])
+            spans = [inner[0], outer_y[other], outer_z[number]]
+            face_x += [
+                send(0, way, spans, has(2, side) & has(1, side_y)) for way in sides
+            ]
+    for number in face_x:
+        received(number)
+    for copy, leaves, _ in copies:
+
+        @pl.when(leaves)
+        def _(copy=copy):
+            copy.wait_send()
+
+
+def exchange(latent, counts):
+    width = latent.shape[-1]
+    sizes = tuple(lax.axis_size(axis) for axis in ("gx", "gy", "gz"))
+    partners = sum(sizes) - 3
+    vmem = pl.BlockSpec(memory_space=pltpu.VMEM)
+    padded = tuple(count + 2 for count in counts) + (CELLS, width)
+    copies = 2 * (1 + 1 + 1 + 2 + 2 + 2 + 4)
+    return pl.pallas_call(
+        functools.partial(exchange_kernel, counts, sizes),
+        out_shape=(
+            jax.ShapeDtypeStruct(padded, jnp.bfloat16),
+            jax.ShapeDtypeStruct((8, width), jnp.float32),
+        ),
+        in_specs=[vmem],
+        out_specs=(vmem, vmem),
+        scratch_shapes=[
+            pltpu.VMEM((3, 8, width), jnp.float32),
+            pltpu.VMEM((partners, 8, width), jnp.float32),
+            pltpu.SemaphoreType.DMA((copies,)),
+            pltpu.SemaphoreType.DMA((copies,)),
+            pltpu.SemaphoreType.DMA((partners,)),
+            pltpu.SemaphoreType.DMA((partners,)),
+        ],
+        compiler_params=pltpu.CompilerParams(
+            collective_id=0, has_side_effects=True, vmem_limit_bytes=32 * 2**20
+        ),
+        cost_estimate=pl.CostEstimate(flops=10**9, bytes_accessed=6 * 10**6, transcendentals=0),
+    )(latent)
 
 
 def attend_kernel(
-    counts, place_ref, limit_ref, x_ref, mean_ref, gain_ref, shift_ref, wqkv_ref, wout_ref,
-    bout_ref, out_ref, k_ref, v_ref, s_ref, top_ref, sum_ref, acc_ref, mix_ref,
+    counts, sizes, limit_ref, x_ref, stats_ref, scale_ref, shift_ref, wqkv_ref, wout_ref,
+    bout_ref, out_ref, mean_ref, gain_ref, k_ref, v_ref, s_ref, top_ref, sum_ref, acc_ref, mix_ref,
 ):
     count_x, count_y, count_z = counts
     pad_y, pad_z = count_y + 2, count_z + 2
@@ -52,15 +229,33 @@
     keys = CHUNK * CELLS
     factor = head_dim ** (-0.5) * math.log2(math.e)
 
+    per = width // GROUPS
+    group = lax.broadcasted_iota(jnp.int32, (width, width), 0) // per
+    member = (group == lax.broadcasted_iota(jnp.int32, (width, width), 1) // per).astype(jnp.float32)
+
+    def group_mean(row):
+        whole = jnp.broadcast_to(row, (8, width))
+        return jnp.dot(
+            whole, member, precision=lax.Precision.HIGHEST, preferred_element_type=jnp.float32
+        )[0:1] / per
+
+    mean = group_mean(stats_ref[0:1, :])
+    apart = stats_ref[0:1, :] - mean
+    var = group_mean(stats_ref[1:2, :] + apart * apart)
+    mean_ref[...] = mean
+    gain_ref[...] = lax.rsqrt(var + 1e-06) * scale_ref[...]
+
     def normed(x):
         scaled = (x.astype(jnp.float32) - mean_ref[...]) * gain_ref[...]
         return (scaled + shift_ref[...]).astype(jnp.bfloat16)
 
+    place = [lax.axis_index(axis) * n for axis, n in zip(("gx", "gy", "gz"), counts)]
+
     def low(axis, index):
-        return jnp.where(place_ref[axis] + index > 0, index, index + 1)
+        return jnp.where(place[axis] + index > 0, index, index + 1)
 
     def high(axis, index):
-        return jnp.where(place_ref[axis] + index + 1 < place_ref[3 + axis], index + 2, index + 1)
+        return jnp.where(place[axis] + index + 1 < counts[axis] * sizes[axis], index + 2, index + 1)
 
     first_x, last_x = low(0, 0), high(0, count_x - 1)
     first_y, last_y = low(1, 0), high(1, count_y - 1)
@@ -90,7 +285,7 @@
     lane_head = lax.broadcasted_iota(jnp.int32, (CELLS, width), 1) // head_dim
 
     def one_block(block_x, block_y, block_z):
-        limit = limit_ref[(block_x * count_y + block_y) * count_z + block_z]
+        limit = limit_ref[block_x, block_y, block_z]
         lo_x, hi_x = low(0, block_x), high(0, block_x)
         lo_y, hi_y = low(1, block_y), high(1, block_y)
         lo_z = jnp.where(limit > 0, low(2, block_z), block_z + 1)
@@ -178,11 +373,7 @@
         return mixed.astype(jnp.bfloat16)
 
     slab = count_z * CELLS
-    natural = lax.broadcasted_iota(jnp.int32, (slab, slab), 0)
-    blocked = lax.broadcasted_iota(jnp.int32, (slab, slab), 1)
-    depth = natural % (count_z * 4)
-    moved = depth // 4 * CELLS + natural // (count_z * 4) * 4 + depth % 4
-    order = (moved == blocked).astype(jnp.bfloat16)
+    order = cell_order(slab, True)
 
     def one_column(index, carry):
         block_x, block_y = index // count_y, index % count_y
@@ -206,22 +397,25 @@
     lax.fori_loop(0, count_x * count_y, one_column, 0)
 
 
-def attend(place, limit, padded, mean, gain, shift, w_qkv, w_out, b_out):
+def attend(limit, padded, stats, gain, shift, w_qkv, w_out, b_out):
     counts = limit.shape
     width = padded.shape[-1]
     flat = padded.reshape(-1, width)
     rows = HEADS * CELLS
+    sizes = tuple(lax.axis_size(axis) for axis in ("gx", "gy", "gz"))
     most = -(-27 // CHUNK)
     smem = pl.BlockSpec(memory_space=pltpu.SMEM)
     vmem = pl.BlockSpec(memory_space=pltpu.VMEM)
     return pl.pallas_call(
-        functools.partial(attend_kernel, counts),
+        functools.partial(attend_kernel, counts, sizes),
         out_shape=jax.ShapeDtypeStruct(
             (counts[0] * 4, counts[1] * 4, counts[2] * 4, width), jnp.bfloat16
         ),
-        in_specs=[smem, smem] + [vmem] * 7,
+        in_specs=[smem] + [vmem] * 7,
         out_specs=vmem,
         scratch_shapes=[
+            pltpu.VMEM((1, width), jnp.float32),
+            pltpu.VMEM((1, width), jnp.float32),
             pltpu.VMEM(flat.shape, jnp.bfloat16),
             pltpu.VMEM(flat.shape, jnp.bfloat16),
             pltpu.VMEM((most, rows, CHUNK * CELLS), jnp.float32),
@@ -234,31 +428,13 @@
         cost_estimate=pl.CostEstimate(
             flops=30 * 10**9, bytes_accessed=7 * 10**6, transcendentals=28 * 10**6
         ),
-    )(place, limit.reshape(-1), flat, mean, gain, shift, w_qkv, w_out, b_out)
+    )(limit, flat, stats, gain, shift, w_qkv, w_out, b_out)
 
 
 def on_device(latent, norm_gain, norm_shift, w_qkv, w_out, b_out, depth_limit):
-    width = latent.shape[-1]
-    per = width // GROUPS
-    axes = ("gx", "gy", "gz")
-    grouped = latent.astype(jnp.float32).reshape(-1, GROUPS, per)
-    count = grouped.shape[0] * per
-    mean_here = jnp.sum(grouped, axis=(0, 2)) / count
-    centred = grouped - mean_here[None, :, None]
-    square_here = jnp.sum(centred * centred, axis=(0, 2)) / count
-    parts = lax.all_gather(jnp.stack([mean_here, square_here]), axes)
-    mean = jnp.mean(parts[:, 0], axis=0)
-    var = jnp.mean(parts[:, 1] + (parts[:, 0] - mean) ** 2, axis=0)
-    gain = jnp.repeat(lax.rsqrt(var + 1e-06), per) * norm_gain
-    padded = halo(to_blocks(latent), (("gy", 1), ("gz", 2), ("gx", 0)))
-    counts = depth_limit.shape
-    place = jnp.stack(
-        [lax.axis_index(axis) * n for axis, n in zip(axes, counts)]
-        + [jnp.int32(lax.axis_size(axis) * n) for axis, n in zip(axes, counts)]
-    ).astype(jnp.int32)
+    padded, stats = exchange(latent, depth_limit.shape)
     return attend(
-        place, depth_limit, padded, jnp.repeat(mean, per)[None], gain[None], norm_shift[None],
-        w_qkv, w_out, b_out[None],
+        depth_limit, padded, stats, norm_gain[None], norm_shift[None], w_qkv, w_out, b_out[None]
     )
 
 

time: 212 us -> 127 us (0.60)
  the two profiles are of different devices: /device:TPU:20 before, /device:TPU:18 now
where the time goes in v2:
time: 127 us; the launch traced here: 125 us
  Pallas kernels  119 us (94%)
  local copies, waits for them, and re-layouts  5.84 us (5%)
    pallas_call x1, Pallas kernels, attend(): pl.pallas_call(functools.partial(attend_kernel, counts, sizes), out_shape...  97.9 us
    pallas_call x1, Pallas kernels, exchange(): pl.pallas_call(functools.partial(exchange_kernel, counts, sizes), out_sha...  21.2 us
    unnamed x14, local copies, waits for them, and re-layouts  5.84 us

profile of v2, /device:TPU:18, one launch (start us, length us, event | category | flops | bytes accessed | tf_op | source)
XLA Modules:
  0.0 125.0 jit_solution(18196780837872676930)
XLA Ops:
  0.0 0.0 copy-start
  0.0 1.2 copy-done
  1.2 21.2 %shard_map.73 = (bf16[4,6,6,64,256]{4,3,2,1,0:T(8,128)(2,1)S(1)}, f32[8,256]{1,0:T(8,128)S(1)}) custom-call(bf16[8,16,16,256]{3,2,1,0:T(8,128)(2,1)S(1)} %copy-done), custom_call_target="tpu_custom_call" | custom-call | flops 1000000000 | bytes 6000000 | tf_op jit(solution)/shard_map/pallas_call | solution.py:197
  22.4 0.0 copy-start.1
  22.4 1.0 copy-done.1
  23.4 0.0 copy-start.2
  23.4 0.9 copy-done.2
  24.3 0.0 copy-start.3
  24.3 0.7 copy-done.3
  25.0 0.0 copy-start.4
  25.0 0.7 copy-done.4
  25.7 0.0 copy-start.5
  25.7 0.7 copy-done.5
  26.4 0.0 copy-start.6
  26.4 0.7 copy-done.6
  27.0 97.9 %shard_map.74 = bf16[8,16,16,256]{3,2,1,0:T(8,128)(2,1)} custom-call(s32[2,4,4]{2,1,0:T(4,128)S(1)} %copy-done.3, bf16[9216,256]{1,0:T(8,128)(2,1)S(1)} %bitcast.7, f32[8,256]{1,0:T(8,128)S(1)} %get-tuple-element.8.stats_ref, f32[1,256]{1,0:T(1,128)S(1)} %bitcast.4, f32[1,256]{1,0:T(1,128)S(1)} %bitcast.5, bf16[256,768]{1,0:T(8,128)(2,1)S(1)} %copy-done.1, ...), custom_call_target="tpu_custom_call" | custom-call | flops 30000001024 | bytes 7000000 | tf_op jit(solution)/shard_map/pallas_call | solution.py:409
Async XLA Ops:
  0.0 1.2 copy-start
  22.4 1.0 copy-start.1
  23.4 0.9 copy-start.2
  24.3 0.7 copy-start.3
  25.0 0.7 copy-start.4
  25.7 0.7 copy-start.5
  26.4 0.7 copy-start.6

commit v3 on v2

--- a/solution.py
+++ b/solution.py
@@ -219,13 +219,12 @@
 
 def attend_kernel(
     counts, sizes, limit_ref, x_ref, stats_ref, scale_ref, shift_ref, wqkv_ref, wout_ref,
-    bout_ref, out_ref, mean_ref, gain_ref, k_ref, v_ref, s_ref, top_ref, sum_ref, acc_ref, mix_ref,
+    bout_ref, out_ref, mean_ref, gain_ref, q_ref, k_ref, v_ref, s_ref, p_ref, mix_ref,
 ):
     count_x, count_y, count_z = counts
     pad_y, pad_z = count_y + 2, count_z + 2
     width = x_ref.shape[1]
     head_dim = width // HEADS
-    rows = HEADS * CELLS
     keys = CHUNK * CELLS
     factor = head_dim ** (-0.5) * math.log2(math.e)
 
@@ -260,6 +259,9 @@
     first_x, last_x = low(0, 0), high(0, count_x - 1)
     first_y, last_y = low(1, 0), high(1, count_y - 1)
     column = pad_z * CELLS
+
+    def flat(at_x, at_y, at_z):
+        return (at_x * pad_y + at_y) * pad_z + at_z
 
     def project(index, carry):
         index_x, index_y = index // pad_y, index % pad_y
@@ -282,7 +284,72 @@
 
     lax.fori_loop(0, (count_x + 2) * pad_y, project, 0)
 
-    lane_head = lax.broadcasted_iota(jnp.int32, (CELLS, width), 1) // head_dim
+    slab = count_z * CELLS
+
+    def project_query(index, carry):
+        source = flat(index // count_y + 1, index % count_y + 1, 1) * CELLS
+        cells = normed(x_ref[pl.ds(pl.multiple_of(source, CELLS), slab), :])
+        q_ref[pl.ds(pl.multiple_of(index * slab, slab), slab), :] = jnp.dot(
+            cells, wqkv_ref[:, :width], preferred_element_type=jnp.float32
+        ).astype(jnp.bfloat16)
+        return carry
+
+    lax.fori_loop(0, count_x * count_y, project_query, 0)
+
+    half = width // 2
+    together = HEADS // 2
+    lane_head = lax.broadcasted_iota(jnp.int32, (CELLS, half), 1) // head_dim
+
+    def attend_block(chunks, masked, own, target, start, ends, total):
+        lo_x, lo_y, lo_z = start
+        hi_x, hi_y, hi_z = ends
+        at_x, at_y, at_z = start
+        spans = []
+        for _ in range(chunks * CHUNK):
+            spans.append(pl.ds(pl.multiple_of(flat(at_x, at_y, at_z) * CELLS, CELLS), CELLS))
+            turn_z = at_z == hi_z
+            at_z = jnp.where(turn_z, lo_z, at_z + 1)
+            turn_y = turn_z & (at_y == hi_y)
+            at_y = jnp.where(turn_y, lo_y, jnp.where(turn_z, at_y + 1, at_y))
+            at_x = jnp.where(turn_y, jnp.minimum(at_x + 1, hi_x), at_x)
+        span = pl.ds(pl.multiple_of(own, CELLS), CELLS)
+        channels = [slice(group * half, (group + 1) * half) for group in range(2)]
+        for group in range(2):
+            query = q_ref[span, channels[group]]
+            stacked = jnp.concatenate(
+                [jnp.where(lane_head == head, query, 0) for head in range(together)], axis=0
+            )
+            for index in range(chunks):
+                chunk = jnp.concatenate(
+                    [k_ref[part, channels[group]] for part in spans[index * CHUNK :][:CHUNK]], axis=0
+                )
+                scores = lax.dot_general(
+                    stacked, chunk, (((1,), (1,)), ((), ())), preferred_element_type=jnp.float32
+                )
+                if index >= masked:
+                    lane = lax.broadcasted_iota(jnp.int32, (1, keys), 1) + index * keys
+                    scores = jnp.where(lane < total * CELLS, scores, LOW)
+                s_ref[group, :, index * keys : (index + 1) * keys] = scores
+        for group in range(2):
+            shares = []
+            for head in range(together):
+                rows = slice(head * CELLS, (head + 1) * CELLS)
+                scores = s_ref[group, rows, : chunks * keys]
+                top = jnp.max(scores, axis=1, keepdims=True) * factor
+                weights = jnp.exp2(scores * factor - top)
+                shares.append(1.0 / jnp.sum(weights, axis=1, keepdims=True))
+                p_ref[group, rows, : chunks * keys] = weights.astype(jnp.bfloat16)
+            values = jnp.concatenate([v_ref[part, channels[group]] for part in spans], axis=0)
+            summed = jnp.dot(
+                p_ref[group, :, : chunks * keys], values, preferred_element_type=jnp.float32
+            )
+            mixed = jnp.zeros((CELLS, half), jnp.float32)
+            for head in range(together):
+                rows = slice(head * CELLS, (head + 1) * CELLS)
+                mixed = jnp.where(lane_head == head, summed[rows] * shares[head], mixed)
+            mix_ref[target, channels[group]] = mixed.astype(jnp.bfloat16)
+
+    forms = ((2, 0), (3, 2), (5, 4), (7, 6))
 
     def one_block(block_x, block_y, block_z):
         limit = limit_ref[block_x, block_y, block_z]
@@ -291,96 +358,26 @@
         lo_z = jnp.where(limit > 0, low(2, block_z), block_z + 1)
         hi_z = jnp.where(limit > 0, high(2, block_z), block_z + 1)
         total = (hi_x - lo_x + 1) * (hi_y - lo_y + 1) * (hi_z - lo_z + 1)
-        full = total // CHUNK
-        chunks = (total + CHUNK - 1) // CHUNK
-        start = (lo_x, lo_y, lo_z)
-
-        def flat(at_x, at_y, at_z):
-            return (at_x * pad_y + at_y) * pad_z + at_z
-
-        def gather(ref, at):
-            pieces = []
-            at_x, at_y, at_z = at
-            for _ in range(CHUNK):
-                index = pl.multiple_of(flat(at_x, at_y, at_z) * CELLS, CELLS)
-                pieces.append(ref[pl.ds(index, CELLS), :])
-                turn_z = at_z == hi_z
-                at_z = jnp.where(turn_z, lo_z, at_z + 1)
-                turn_y = turn_z & (at_y == hi_y)
-                at_y = jnp.where(turn_y, lo_y, jnp.where(turn_z, at_y + 1, at_y))
-                at_x = jnp.where(turn_y, jnp.minimum(at_x + 1, hi_x), at_x)
-            return jnp.concatenate(pieces, axis=0), (at_x, at_y, at_z)
-
-        own = pl.multiple_of(flat(block_x + 1, block_y + 1, block_z + 1) * CELLS, CELLS)
-        query = jnp.dot(
-            normed(x_ref[pl.ds(own, CELLS), :]),
-            wqkv_ref[:, :width],
-            preferred_element_type=jnp.float32,
-        )
-        stacked = jnp.concatenate(
-            [jnp.where(lane_head == head, query, 0.0).astype(jnp.bfloat16) for head in range(HEADS)],
-            axis=0,
-        )
-        top_ref[...] = jnp.full_like(top_ref, LOW)
-
-        def score(index, at, masked):
-            chunk, at = gather(k_ref, at)
-            scores = lax.dot_general(
-                stacked, chunk, (((1,), (1,)), ((), ())), preferred_element_type=jnp.float32
-            )
-            if masked:
-                lane = lax.broadcasted_iota(jnp.int32, (1, keys), 1) + index * keys
-                scores = jnp.where(lane < total * CELLS, scores, LOW)
-            s_ref[index] = scores
-            best = scores[:, :128]
-            for part in range(1, keys // 128):
-                best = jnp.maximum(best, scores[:, part * 128 : (part + 1) * 128])
-            top_ref[...] = jnp.maximum(top_ref[...], best)
-            return at
-
-        at = lax.fori_loop(0, full, functools.partial(score, masked=False), start)
-
-        @pl.when(chunks > full)
-        def _():
-            score(full, at, True)
-
-        top = jnp.max(top_ref[...], axis=1, keepdims=True) * factor
-        top_ref[...] = jnp.broadcast_to(top, top_ref.shape)
-        sum_ref[...] = jnp.zeros_like(sum_ref)
-        acc_ref[...] = jnp.zeros_like(acc_ref)
-
-        def mix(index, at):
-            chunk, at = gather(v_ref, at)
-            weights = []
-            added = None
-            for part in range(keys // 128):
-                scores = s_ref[index, :, part * 128 : (part + 1) * 128]
-                weight = jnp.exp2(scores * factor - top_ref[...])
-                added = weight if added is None else added + weight
-                weights.append(weight.astype(jnp.bfloat16))
-            sum_ref[...] += added
-            acc_ref[...] += jnp.dot(
-                jnp.concatenate(weights, axis=1), chunk, preferred_element_type=jnp.float32
-            )
-            return at
-
-        lax.fori_loop(0, chunks, mix, start)
-        share = 1.0 / jnp.sum(sum_ref[...], axis=1, keepdims=True)
-        mixed = jnp.zeros((CELLS, width), jnp.float32)
-        for head in range(HEADS):
-            part = slice(head * CELLS, (head + 1) * CELLS)
-            mixed = jnp.where(lane_head == head, acc_ref[part, :] * share[part], mixed)
-        return mixed.astype(jnp.bfloat16)
-
-    slab = count_z * CELLS
+        own = ((block_x * count_y + block_y) * count_z + block_z) * CELLS
+        target = pl.ds(pl.multiple_of(block_z * CELLS, CELLS), CELLS)
+        below = 0
+        for chunks, masked in forms:
+
+            @pl.when((total > below * CHUNK) & (total <= chunks * CHUNK))
+            def _(chunks=chunks, masked=masked):
+                attend_block(
+                    chunks, masked, own, target, (lo_x, lo_y, lo_z), (hi_x, hi_y, hi_z), total
+                )
+
+            below = chunks
+
     order = cell_order(slab, True)
 
     def one_column(index, carry):
         block_x, block_y = index // count_y, index % count_y
 
         def one_depth(block_z, carry):
-            span = pl.ds(pl.multiple_of(block_z * CELLS, CELLS), CELLS)
-            mix_ref[span, :] = one_block(block_x, block_y, block_z)
+            one_block(block_x, block_y, block_z)
             return carry
 
         lax.fori_loop(0, count_z, one_depth, 0)
@@ -416,12 +413,11 @@
         scratch_shapes=[
             pltpu.VMEM((1, width), jnp.float32),
             pltpu.VMEM((1, width), jnp.float32),
+            pltpu.VMEM((counts[0] * counts[1] * counts[2] * CELLS, width), jnp.bfloat16),
             pltpu.VMEM(flat.shape, jnp.bfloat16),
             pltpu.VMEM(flat.shape, jnp.bfloat16),
-            pltpu.VMEM((most, rows, CHUNK * CELLS), jnp.float32),
-            pltpu.VMEM((rows, 128), jnp.float32),
-            pltpu.VMEM((rows, 128), jnp.float32),
-            pltpu.VMEM((rows, width), jnp.float32),
+            pltpu.VMEM((2, rows // 2, most * CHUNK * CELLS), jnp.float32),
+            pltpu.VMEM((2, rows // 2, most * CHUNK * CELLS), jnp.bfloat16),
             pltpu.VMEM((counts[2] * CELLS, width), jnp.bfloat16),
         ],
         compiler_params=pltpu.CompilerParams(vmem_limit_bytes=48 * 2**20),

time: 127 us -> 84.6 us (0.67)
  the two profiles are of different devices: /device:TPU:18 before, /device:TPU:13 now
where the time goes in v3:
time: 84.6 us; the launch traced here: 84.1 us
  Pallas kernels  78.3 us (93%)
  local copies, waits for them, and re-layouts  5.84 us (7%)
    pallas_call x1, Pallas kernels, attend(): pl.pallas_call(functools.partial(attend_kernel, counts, sizes), out_shape...  55.2 us
    pallas_call x1, Pallas kernels, exchange(): pl.pallas_call(functools.partial(exchange_kernel, counts, sizes), out_sha...  23 us
    unnamed x14, local copies, waits for them, and re-layouts  5.84 us

profile of v3, /device:TPU:13, one launch (start us, length us, event | category | flops | bytes accessed | tf_op | source)
XLA Modules:
  0.0 84.1 jit_solution(11835076850451331882)
XLA Ops:
  0.0 0.0 copy-start
  0.0 1.2 %copy-done = bf16[8,16,16,256]{3,2,1,0:T(8,128)(2,1)S(1)} copy-done((bf16[8,16,16,256]{3,2,1,0:T(8,128)(2,1)S(1)}, bf16[8,16,16,256]{3,2,1,0:T(8,128)(2,1)}, u32[]{:S(2)}) %copy-start) | copy-done | bytes 1048600
  1.2 23.0 %shard_map.73 = (bf16[4,6,6,64,256]{4,3,2,1,0:T(8,128)(2,1)S(1)}, f32[8,256]{1,0:T(8,128)S(1)}) custom-call(bf16[8,16,16,256]{3,2,1,0:T(8,128)(2,1)S(1)} %copy-done), custom_call_target="tpu_custom_call" | custom-call | flops 1000000000 | bytes 6000000 | tf_op jit(solution)/shard_map/pallas_call | solution.py:197
  24.2 0.0 copy-start.1
  24.3 1.0 %copy-done.1 = bf16[256,768]{1,0:T(8,128)(2,1)S(1)} copy-done((bf16[256,768]{1,0:T(8,128)(2,1)S(1)}, bf16[256,768]{1,0:T(8,128)(2,1)}, u32[]{:S(2)}) %copy-start.1) | copy-done | bytes 393240
  25.2 0.0 copy-start.2
  25.2 0.9 %copy-done.2 = bf16[256,256]{1,0:T(8,128)(2,1)S(1)} copy-done((bf16[256,256]{1,0:T(8,128)(2,1)S(1)}, bf16[256,256]{1,0:T(8,128)(2,1)}, u32[]{:S(2)}) %copy-start.2) | copy-done | bytes 131096
  26.1 0.0 copy-start.3
  26.1 0.7 copy-done.3
  26.8 0.0 copy-start.4
  26.8 0.7 copy-done.4
  27.5 0.0 copy-start.5
  27.5 0.7 copy-done.5
  28.2 0.0 copy-start.6
  28.2 0.7 copy-done.6
  28.9 55.2 %shard_map.74 = bf16[8,16,16,256]{3,2,1,0:T(8,128)(2,1)} custom-call(s32[2,4,4]{2,1,0:T(4,128)S(1)} %copy-done.3, bf16[9216,256]{1,0:T(8,128)(2,1)S(1)} %bitcast.7, f32[8,256]{1,0:T(8,128)S(1)} %get-tuple-element.8.stats_ref, f32[1,256]{1,0:T(1,128)S(1)} %bitcast.4, f32[1,256]{1,0:T(1,128)S(1)} %bitcast.5, bf16[256,768]{1,0:T(8,128)(2,1)S(1)} %copy-done.1, ...), custom_call_target="tpu_custom_call" | custom-call | flops 30000001024 | bytes 7000000 | tf_op jit(solution)/shard_map/pallas_call | solution.py:406
Async XLA Ops:
  0.0 1.2 %copy-start = (bf16[8,16,16,256]{3,2,1,0:T(8,128)(2,1)S(1)}, bf16[8,16,16,256]{3,2,1,0:T(8,128)(2,1)}, u32[]{:S(2)}) copy-start(bf16[8,16,16,256]{3,2,1,0:T(8,128)(2,1)} %latent_ref.1) | copy-start | bytes 3145732
  24.2 1.0 %copy-start.1 = (bf16[256,768]{1,0:T(8,128)(2,1)S(1)}, bf16[256,768]{1,0:T(8,128)(2,1)}, u32[]{:S(2)}) copy-start(bf16[256,768]{1,0:T(8,128)(2,1)} %wqkv_ref.1) | copy-start | bytes 1179652
  25.2 0.9 %copy-start.2 = (bf16[256,256]{1,0:T(8,128)(2,1)S(1)}, bf16[256,256]{1,0:T(8,128)(2,1)}, u32[]{:S(2)}) copy-start(bf16[256,256]{1,0:T(8,128)(2,1)} %wout_ref.1) | copy-start | bytes 393220
  26.1 0.7 copy-start.3
  26.8 0.7 copy-start.4
  27.5 0.7 copy-start.5
  28.2 0.7 copy-start.6

commit v4 on v3

--- a/solution.py
+++ b/solution.py
@@ -219,7 +219,7 @@
 
 def attend_kernel(
     counts, sizes, limit_ref, x_ref, stats_ref, scale_ref, shift_ref, wqkv_ref, wout_ref,
-    bout_ref, out_ref, mean_ref, gain_ref, q_ref, k_ref, v_ref, s_ref, p_ref, mix_ref,
+    bout_ref, out_ref, mean_ref, gain_ref, q_ref, k_ref, v_ref, s_ref, p_ref, top_ref, mix_ref,
 ):
     count_x, count_y, count_z = counts
     pad_y, pad_z = count_y + 2, count_z + 2
@@ -314,40 +314,67 @@
             at_x = jnp.where(turn_y, jnp.minimum(at_x + 1, hi_x), at_x)
         span = pl.ds(pl.multiple_of(own, CELLS), CELLS)
         channels = [slice(group * half, (group + 1) * half) for group in range(2)]
-        for group in range(2):
+        lanes = [slice(part * 128, (part + 1) * 128) for part in range(chunks * keys // 128)]
+
+        def score(group, stacked, index, best):
+            chunk = jnp.concatenate(
+                [k_ref[part, channels[group]] for part in spans[index * CHUNK :][:CHUNK]], axis=0
+            )
+            scores = lax.dot_general(
+                stacked, chunk, (((1,), (1,)), ((), ())), preferred_element_type=jnp.float32
+            )
+            if index >= masked:
+                lane = lax.broadcasted_iota(jnp.int32, (1, keys), 1) + index * keys
+                scores = jnp.where(lane < total * CELLS, scores, LOW)
+            s_ref[group, :, index * keys : (index + 1) * keys] = scores
+            for part in range(keys // 128):
+                piece = scores[:, part * 128 : (part + 1) * 128]
+                best = piece if best is None else jnp.maximum(best, piece)
+            return best
+
+        def stack(group):
             query = q_ref[span, channels[group]]
-            stacked = jnp.concatenate(
+            return jnp.concatenate(
                 [jnp.where(lane_head == head, query, 0) for head in range(together)], axis=0
             )
-            for index in range(chunks):
-                chunk = jnp.concatenate(
-                    [k_ref[part, channels[group]] for part in spans[index * CHUNK :][:CHUNK]], axis=0
-                )
-                scores = lax.dot_general(
-                    stacked, chunk, (((1,), (1,)), ((), ())), preferred_element_type=jnp.float32
-                )
-                if index >= masked:
-                    lane = lax.broadcasted_iota(jnp.int32, (1, keys), 1) + index * keys
-                    scores = jnp.where(lane < total * CELLS, scores, LOW)
-                s_ref[group, :, index * keys : (index + 1) * keys] = scores
-        for group in range(2):
-            shares = []
-            for head in range(together):
-                rows = slice(head * CELLS, (head + 1) * CELLS)
-                scores = s_ref[group, rows, : chunks * keys]
-                top = jnp.max(scores, axis=1, keepdims=True) * factor
-                weights = jnp.exp2(scores * factor - top)
-                shares.append(1.0 / jnp.sum(weights, axis=1, keepdims=True))
-                p_ref[group, rows, : chunks * keys] = weights.astype(jnp.bfloat16)
+
+        def keep_top(group, best):
+            top = jnp.max(best, axis=1, keepdims=True) * factor
+            top_ref[group] = jnp.broadcast_to(top, best.shape)
+
+        def weigh(group, index):
+            for lane in lanes[index * (keys // 128) : (index + 1) * (keys // 128)]:
+                weights = jnp.exp2(s_ref[group, :, lane] * factor - top_ref[group])
+                p_ref[group, :, lane] = weights.astype(jnp.bfloat16)
+
+        def mix(group):
             values = jnp.concatenate([v_ref[part, channels[group]] for part in spans], axis=0)
             summed = jnp.dot(
-                p_ref[group, :, : chunks * keys], values, preferred_element_type=jnp.float32
+                p_ref[group, :, : chunks * keys],
+                jnp.concatenate([values, jnp.ones_like(values)], axis=1),
+                preferred_element_type=jnp.float32,
             )
             mixed = jnp.zeros((CELLS, half), jnp.float32)
             for head in range(together):
                 rows = slice(head * CELLS, (head + 1) * CELLS)
-                mixed = jnp.where(lane_head == head, summed[rows] * shares[head], mixed)
+                mixed = jnp.where(lane_head == head, summed[rows, :half] / summed[rows, half:], mixed)
             mix_ref[target, channels[group]] = mixed.astype(jnp.bfloat16)
+
+        stacked = stack(0)
+        best = None
+        for index in range(chunks):
+            best = score(0, stacked, index, best)
+        keep_top(0, best)
+        stacked = stack(1)
+        best = None
+        for index in range(chunks):
+            best = score(1, stacked, index, best)
+            weigh(0, index)
+        keep_top(1, best)
+        mix(0)
+        for index in range(chunks):
+            weigh(1, index)
+        mix(1)
 
     forms = ((2, 0), (3, 2), (5, 4), (7, 6))
 
@@ -418,6 +445,7 @@
             pltpu.VMEM(flat.shape, jnp.bfloat16),
             pltpu.VMEM((2, rows // 2, most * CHUNK * CELLS), jnp.float32),
             pltpu.VMEM((2, rows // 2, most * CHUNK * CELLS), jnp.bfloat16),
+            pltpu.VMEM((2, rows // 2, 128), jnp.float32),
             pltpu.VMEM((counts[2] * CELLS, width), jnp.bfloat16),
         ],
         compiler_params=pltpu.CompilerParams(vmem_limit_bytes=48 * 2**20),

time: 84.6 us -> 87.8 us (1.038); the launches traced: 84.1 us -> 88.2 us
  Pallas kernels: 78.3 us -> 82.4 us
    pallas_call x1, Pallas kernels: 55.2 us -> 59.3 us  [attend(): pl.pallas_call(functools.partial(attend_kernel, counts, sizes), out_shape...]
where the time goes in v4:
time: 87.8 us; the launch traced here: 88.2 us
  Pallas kernels  82.4 us (94%)
  local copies, waits for them, and re-layouts  5.84 us (7%)
    pallas_call x1, Pallas kernels, attend(): pl.pallas_call(functools.partial(attend_kernel, counts, sizes), out_shape...  59.3 us
    pallas_call x1, Pallas kernels, exchange(): pl.pallas_call(functools.partial(exchange_kernel, counts, sizes), out_sha...  23 us
    unnamed x14, local copies, waits for them, and re-layouts  5.84 us

profile of v4, /device:TPU:13, one launch (start us, length us, event | category | flops | bytes accessed | tf_op | source)
XLA Modules:
  0.0 88.2 jit_solution(15585721868627251222)
XLA Ops:
  0.0 0.0 copy-start
  0.0 1.2 %copy-done = bf16[8,16,16,256]{3,2,1,0:T(8,128)(2,1)S(1)} copy-done((bf16[8,16,16,256]{3,2,1,0:T(8,128)(2,1)S(1)}, bf16[8,16,16,256]{3,2,1,0:T(8,128)(2,1)}, u32[]{:S(2)}) %copy-start) | copy-done | bytes 1048600
  1.2 23.0 %shard_map.73 = (bf16[4,6,6,64,256]{4,3,2,1,0:T(8,128)(2,1)S(1)}, f32[8,256]{1,0:T(8,128)S(1)}) custom-call(bf16[8,16,16,256]{3,2,1,0:T(8,128)(2,1)S(1)} %copy-done), custom_call_target="tpu_custom_call" | custom-call | flops 1000000000 | bytes 6000000 | tf_op jit(solution)/shard_map/pallas_call | solution.py:197
  24.2 0.0 copy-start.1
  24.3 1.0 %copy-done.1 = bf16[256,768]{1,0:T(8,128)(2,1)S(1)} copy-done((bf16[256,768]{1,0:T(8,128)(2,1)S(1)}, bf16[256,768]{1,0:T(8,128)(2,1)}, u32[]{:S(2)}) %copy-start.1) | copy-done | bytes 393240
  25.2 0.0 copy-start.2
  25.2 0.9 %copy-done.2 = bf16[256,256]{1,0:T(8,128)(2,1)S(1)} copy-done((bf16[256,256]{1,0:T(8,128)(2,1)S(1)}, bf16[256,256]{1,0:T(8,128)(2,1)}, u32[]{:S(2)}) %copy-start.2) | copy-done | bytes 131096
  26.1 0.0 copy-start.3
  26.1 0.7 copy-done.3
  26.8 0.0 copy-start.4
  26.8 0.7 copy-done.4
  27.5 0.0 copy-start.5
  27.5 0.7 copy-done.5
  28.2 0.0 copy-start.6
  28.2 0.7 copy-done.6
  28.9 59.3 %shard_map.74 = bf16[8,16,16,256]{3,2,1,0:T(8,128)(2,1)} custom-call(s32[2,4,4]{2,1,0:T(4,128)S(1)} %copy-done.3, bf16[9216,256]{1,0:T(8,128)(2,1)S(1)} %bitcast.7, f32[8,256]{1,0:T(8,128)S(1)} %get-tuple-element.8.stats_ref, f32[1,256]{1,0:T(1,128)S(1)} %bitcast.4, f32[1,256]{1,0:T(1,128)S(1)} %bitcast.5, bf16[256,768]{1,0:T(8,128)(2,1)S(1)} %copy-done.1, ...), custom_call_target="tpu_custom_call" | custom-call | flops 30000001024 | bytes 7000000 | tf_op jit(solution)/shard_map/pallas_call | solution.py:433
Async XLA Ops:
  0.0 1.2 %copy-start = (bf16[8,16,16,256]{3,2,1,0:T(8,128)(2,1)S(1)}, bf16[8,16,16,256]{3,2,1,0:T(8,128)(2,1)}, u32[]{:S(2)}) copy-start(bf16[8,16,16,256]{3,2,1,0:T(8,128)(2,1)} %latent_ref.1) | copy-start | bytes 3145732
  24.2 1.0 %copy-start.1 = (bf16[256,768]{1,0:T(8,128)(2,1)S(1)}, bf16[256,768]{1,0:T(8,128)(2,1)}, u32[]{:S(2)}) copy-start(bf16[256,768]{1,0:T(8,128)(2,1)} %wqkv_ref.1) | copy-start | bytes 1179652
  25.2 0.9 %copy-start.2 = (bf16[256,256]{1,0:T(8,128)(2,1)S(1)}, bf16[256,256]{1,0:T(8,128)(2,1)}, u32[]{:S(2)}) copy-start(bf16[256,256]{1,0:T(8,128)(2,1)} %wout_ref.1) | copy-start | bytes 393220
  26.1 0.7 copy-start.3
  26.8 0.7 copy-start.4
  27.5 0.7 copy-start.5
  28.2 0.7 copy-start.6

commit v5 on v3

--- a/solution.py
+++ b/solution.py
@@ -11,8 +11,7 @@
 HEADS = 8
 GROUPS = 32
 CELLS = 64
-CHUNK = 4
-LOW = -1e30
+PIECE = 9
 
 
 def cell_order(slab, inverse):
@@ -225,7 +224,6 @@
     pad_y, pad_z = count_y + 2, count_z + 2
     width = x_ref.shape[1]
     head_dim = width // HEADS
-    keys = CHUNK * CELLS
     factor = head_dim ** (-0.5) * math.log2(math.e)
 
     per = width // GROUPS
@@ -299,13 +297,19 @@
     half = width // 2
     together = HEADS // 2
     lane_head = lax.broadcasted_iota(jnp.int32, (CELLS, half), 1) // head_dim
-
-    def attend_block(chunks, masked, own, target, start, ends, total):
+    stack = together * CELLS
+    row_of = lax.broadcasted_iota(jnp.int32, (half, stack), 0) // head_dim
+    column_of = lax.broadcasted_iota(jnp.int32, (half, stack), 1) // CELLS
+    diagonal = row_of == column_of
+    cell = lax.broadcasted_iota(jnp.int32, (CELLS, stack), 0)
+    fold = (cell == lax.broadcasted_iota(jnp.int32, (CELLS, stack), 1) % CELLS).astype(jnp.bfloat16)
+
+    def attend_block(blocks, own, target, start, ends):
         lo_x, lo_y, lo_z = start
         hi_x, hi_y, hi_z = ends
         at_x, at_y, at_z = start
         spans = []
-        for _ in range(chunks * CHUNK):
+        for _ in range(blocks):
             spans.append(pl.ds(pl.multiple_of(flat(at_x, at_y, at_z) * CELLS, CELLS), CELLS))
             turn_z = at_z == hi_z
             at_z = jnp.where(turn_z, lo_z, at_z + 1)
@@ -314,42 +318,47 @@
             at_x = jnp.where(turn_y, jnp.minimum(at_x + 1, hi_x), at_x)
         span = pl.ds(pl.multiple_of(own, CELLS), CELLS)
         channels = [slice(group * half, (group + 1) * half) for group in range(2)]
+        tops = []
         for group in range(2):
             query = q_ref[span, channels[group]]
             stacked = jnp.concatenate(
                 [jnp.where(lane_head == head, query, 0) for head in range(together)], axis=0
             )
-            for index in range(chunks):
-                chunk = jnp.concatenate(
-                    [k_ref[part, channels[group]] for part in spans[index * CHUNK :][:CHUNK]], axis=0
+            best = None
+            for first in range(0, blocks, PIECE):
+                part = spans[first : first + PIECE]
+                scores = lax.dot_general(
+                    jnp.concatenate([k_ref[one, channels[group]] for one in part], axis=0),
+                    stacked,
+                    (((1,), (1,)), ((), ())),
+                    preferred_element_type=jnp.float32,
                 )
-                scores = lax.dot_general(
-                    stacked, chunk, (((1,), (1,)), ((), ())), preferred_element_type=jnp.float32
-                )
-                if index >= masked:
-                    lane = lax.broadcasted_iota(jnp.int32, (1, keys), 1) + index * keys
-                    scores = jnp.where(lane < total * CELLS, scores, LOW)
-                s_ref[group, :, index * keys : (index + 1) * keys] = scores
+                s_ref[group, first * CELLS : (first + len(part)) * CELLS, :] = scores
+                for one in range(len(part)):
+                    piece = scores[one * CELLS : (one + 1) * CELLS]
+                    best = piece if best is None else jnp.maximum(best, piece)
+            tops.append(jnp.max(best, axis=0, keepdims=True) * factor)
         for group in range(2):
-            shares = []
-            for head in range(together):
-                rows = slice(head * CELLS, (head + 1) * CELLS)
-                scores = s_ref[group, rows, : chunks * keys]
-                top = jnp.max(scores, axis=1, keepdims=True) * factor
-                weights = jnp.exp2(scores * factor - top)
-                shares.append(1.0 / jnp.sum(weights, axis=1, keepdims=True))
-                p_ref[group, rows, : chunks * keys] = weights.astype(jnp.bfloat16)
-            values = jnp.concatenate([v_ref[part, channels[group]] for part in spans], axis=0)
-            summed = jnp.dot(
-                p_ref[group, :, : chunks * keys], values, preferred_element_type=jnp.float32
+            added = None
+            for index in range(blocks):
+                rows = slice(index * CELLS, (index + 1) * CELLS)
+                weights = jnp.exp2(s_ref[group, rows, :] * factor - tops[group])
+                added = weights if added is None else added + weights
+                p_ref[group, rows, :] = weights.astype(jnp.bfloat16)
+            share = 1.0 / jnp.sum(added, axis=0, keepdims=True)
+            values = jnp.concatenate([v_ref[one, channels[group]] for one in spans], axis=0)
+            summed = lax.dot_general(
+                values,
+                p_ref[group, : blocks * CELLS, :],
+                (((0,), (0,)), ((), ())),
+                preferred_element_type=jnp.float32,
             )
-            mixed = jnp.zeros((CELLS, half), jnp.float32)
-            for head in range(together):
-                rows = slice(head * CELLS, (head + 1) * CELLS)
-                mixed = jnp.where(lane_head == head, summed[rows] * shares[head], mixed)
-            mix_ref[target, channels[group]] = mixed.astype(jnp.bfloat16)
-
-    forms = ((2, 0), (3, 2), (5, 4), (7, 6))
+            mixed = jnp.where(diagonal, summed * share, 0.0).astype(jnp.bfloat16)
+            mix_ref[target, channels[group]] = lax.dot_general(
+                fold, mixed, (((1,), (1,)), ((), ())), preferred_element_type=jnp.float32
+            ).astype(jnp.bfloat16)
+
+    forms = sorted({x * y * z for x in (1, 2, 3) for y in (1, 2, 3) for z in (1, 2, 3)})
 
     def one_block(block_x, block_y, block_z):
         limit = limit_ref[block_x, block_y, block_z]
@@ -360,16 +369,11 @@
         total = (hi_x - lo_x + 1) * (hi_y - lo_y + 1) * (hi_z - lo_z + 1)
         own = ((block_x * count_y + block_y) * count_z + block_z) * CELLS
         target = pl.ds(pl.multiple_of(block_z * CELLS, CELLS), CELLS)
-        below = 0
-        for chunks, masked in forms:
-
-            @pl.when((total > below * CHUNK) & (total <= chunks * CHUNK))
-            def _(chunks=chunks, masked=masked):
-                attend_block(
-                    chunks, masked, own, target, (lo_x, lo_y, lo_z), (hi_x, hi_y, hi_z), total
-                )
-
-            below = chunks
+        for blocks in forms:
+
+            @pl.when(total == blocks)
+            def _(blocks=blocks):
+                attend_block(blocks, own, target, (lo_x, lo_y, lo_z), (hi_x, hi_y, hi_z))
 
     order = cell_order(slab, True)
 
@@ -400,7 +404,7 @@
     flat = padded.reshape(-1, width)
     rows = HEADS * CELLS
     sizes = tuple(lax.axis_size(axis) for axis in ("gx", "gy", "gz"))
-    most = -(-27 // CHUNK)
+    most = 27 * CELLS
     smem = pl.BlockSpec(memory_space=pltpu.SMEM)
     vmem = pl.BlockSpec(memory_space=pltpu.VMEM)
     return pl.pallas_call(
@@ -416,8 +420,8 @@
             pltpu.VMEM((counts[0] * counts[1] * counts[2] * CELLS, width), jnp.bfloat16),
             pltpu.VMEM(flat.shape, jnp.bfloat16),
             pltpu.VMEM(flat.shape, jnp.bfloat16),
-            pltpu.VMEM((2, rows // 2, most * CHUNK * CELLS), jnp.float32),
-            pltpu.VMEM((2, rows // 2, most * CHUNK * CELLS), jnp.bfloat16),
+            pltpu.VMEM((2, most, rows // 2), jnp.float32),
+            pltpu.VMEM((2, most, rows // 2), jnp.bfloat16),
             pltpu.VMEM((counts[2] * CELLS, width), jnp.bfloat16),
         ],
         compiler_params=pltpu.CompilerParams(vmem_limit_bytes=48 * 2**20),

time: 84.6 us -> 89 us (1.052)
  the two profiles are of different devices: /device:TPU:13 before, /device:TPU:19 now
where the time goes in v5:
time: 89 us; the launch traced here: 88.9 us
  Pallas kernels  83 us (93%)
  local copies, waits for them, and re-layouts  5.84 us (7%)
    pallas_call x1, Pallas kernels, attend(): pl.pallas_call(functools.partial(attend_kernel, counts, sizes), out_shape...  61.3 us
    pallas_call x1, Pallas kernels, exchange(): pl.pallas_call(functools.partial(exchange_kernel, counts, sizes), out_sha...  21.7 us
    unnamed x14, local copies, waits for them, and re-layouts  5.84 us

profile of v5, /device:TPU:19, one launch (start us, length us, event | category | flops | bytes accessed | tf_op | source)
XLA Modules:
  0.0 88.9 jit_solution(13636995659538566770)
XLA Ops:
  0.0 0.0 copy-start
  0.0 1.2 %copy-done = bf16[8,16,16,256]{3,2,1,0:T(8,128)(2,1)S(1)} copy-done((bf16[8,16,16,256]{3,2,1,0:T(8,128)(2,1)S(1)}, bf16[8,16,16,256]{3,2,1,0:T(8,128)(2,1)}, u32[]{:S(2)}) %copy-start) | copy-done | bytes 1048600
  1.2 21.7 %shard_map.73 = (bf16[4,6,6,64,256]{4,3,2,1,0:T(8,128)(2,1)S(1)}, f32[8,256]{1,0:T(8,128)S(1)}) custom-call(bf16[8,16,16,256]{3,2,1,0:T(8,128)(2,1)S(1)} %copy-done), custom_call_target="tpu_custom_call" | custom-call | flops 1000000000 | bytes 6000000 | tf_op jit(solution)/shard_map/pallas_call | solution.py:196
  23.0 0.0 copy-start.1
  23.0 1.0 %copy-done.1 = bf16[256,768]{1,0:T(8,128)(2,1)S(1)} copy-done((bf16[256,768]{1,0:T(8,128)(2,1)S(1)}, bf16[256,768]{1,0:T(8,128)(2,1)}, u32[]{:S(2)}) %copy-start.1) | copy-done | bytes 393240
  24.0 0.0 copy-start.2
  24.0 0.9 %copy-done.2 = bf16[256,256]{1,0:T(8,128)(2,1)S(1)} copy-done((bf16[256,256]{1,0:T(8,128)(2,1)S(1)}, bf16[256,256]{1,0:T(8,128)(2,1)}, u32[]{:S(2)}) %copy-start.2) | copy-done | bytes 131096
  24.9 0.0 copy-start.3
  24.9 0.7 copy-done.3
  25.6 0.0 copy-start.4
  25.6 0.7 copy-done.4
  26.2 0.0 copy-start.5
  26.2 0.7 copy-done.5
  26.9 0.0 copy-start.6
  26.9 0.7 copy-done.6
  27.6 61.3 %shard_map.74 = bf16[8,16,16,256]{3,2,1,0:T(8,128)(2,1)} custom-call(s32[2,4,4]{2,1,0:T(4,128)S(1)} %copy-done.3, bf16[9216,256]{1,0:T(8,128)(2,1)S(1)} %bitcast.7, f32[8,256]{1,0:T(8,128)S(1)} %get-tuple-element.8.stats_ref, f32[1,256]{1,0:T(1,128)S(1)} %bitcast.4, f32[1,256]{1,0:T(1,128)S(1)} %bitcast.5, bf16[256,768]{1,0:T(8,128)(2,1)S(1)} %copy-done.1, ...), custom_call_target="tpu_custom_call" | custom-call | flops 30000001024 | bytes 7000000 | tf_op jit(solution)/shard_map/pallas_call | solution.py:410
Async XLA Ops:
  0.0 1.2 %copy-start = (bf16[8,16,16,256]{3,2,1,0:T(8,128)(2,1)S(1)}, bf16[8,16,16,256]{3,2,1,0:T(8,128)(2,1)}, u32[]{:S(2)}) copy-start(bf16[8,16,16,256]{3,2,1,0:T(8,128)(2,1)} %latent_ref.1) | copy-start | bytes 3145732
  23.0 1.0 %copy-start.1 = (bf16[256,768]{1,0:T(8,128)(2,1)S(1)}, bf16[256,768]{1,0:T(8,128)(2,1)}, u32[]{:S(2)}) copy-start(bf16[256,768]{1,0:T(8,128)(2,1)} %wqkv_ref.1) | copy-start | bytes 1179652
  24.0 0.9 %copy-start.2 = (bf16[256,256]{1,0:T(8,128)(2,1)S(1)}, bf16[256,256]{1,0:T(8,128)(2,1)}, u32[]{:S(2)}) copy-start(bf16[256,256]{1,0:T(8,128)(2,1)} %wout_ref.1) | copy-start | bytes 393220
  24.9 0.7 copy-start.3
  25.6 0.7 copy-start.4
  26.2 0.7 copy-start.5
  26.9 0.7 copy-start.6
